TPU v7x, 32 devices: a whole 2x2x4 slice. The times are simulated.
32 devices in a mesh: dp: 4 (over y, x), fsdp: 8 (over z, core).
Axes of the slice: x: 2, y: 2, z: 4, core: 2. Of those that a mesh axis runs over, the one named last changes fastest.
Arguments:
- latents: bfloat16 [32, 256, 768], P(('dp', 'fsdp')), may hold values from -6 to 6
- conditioning: bfloat16 [32, 768], P(('dp', 'fsdp')), may hold values from -6 to 6
- cotangent: bfloat16 [32, 256, 768], P(('dp', 'fsdp')), may hold values from -6 to 6
- latent_count: int32 [32], P(('dp', 'fsdp')), may hold values from 0 to 1, as said below
- ada_weight: bfloat16 [768, 4608], P('dp', 'fsdp'), may hold values from -0.21875 to 0.21875
- ada_bias: bfloat16 [4608], P('fsdp'), may hold values from -3 to 3
- qkv_weight: bfloat16 [768, 2304], P('dp', 'fsdp'), may hold values from -0.21875 to 0.21875
- qv_bias: bfloat16 [1536], P('fsdp'), may hold values from -3 to 3
- proj_weight: bfloat16 [768, 768], P('dp', 'fsdp'), may hold values from -0.875 to 0.875
- proj_bias: bfloat16 [768], P('fsdp'), may hold values from -3 to 3
- fc1_weight: bfloat16 [768, 3072], P('dp', 'fsdp'), may hold values from -0.21875 to 0.21875
- fc1_bias: bfloat16 [3072], P('fsdp'), may hold values from -3 to 3
- fc2_weight: bfloat16 [3072, 768], P('dp', 'fsdp'), may hold values from -0.109375 to 0.109375
- fc2_bias: bfloat16 [768], P('fsdp'), may hold values from -3 to 3
Outputs:
- block_out: bfloat16 [32, 256, 768], P(('dp', 'fsdp'))
- latents_grad: bfloat16 [32, 256, 768], P(('dp', 'fsdp'))
- conditioning_grad: float32 [32, 768], P(('dp', 'fsdp'))
- ada_weight_grad: float32 [768, 4608], P('dp', 'fsdp')
- ada_bias_grad: float32 [4608], P('fsdp')
- qkv_weight_grad: float32 [768, 2304], P('dp', 'fsdp')
- qv_bias_grad: float32 [1536], P('fsdp')
- proj_weight_grad: float32 [768, 768], P('dp', 'fsdp')
- proj_bias_grad: float32 [768], P('fsdp')
- fc1_weight_grad: float32 [768, 3072], P('dp', 'fsdp')
- fc1_bias_grad: float32 [3072], P('fsdp')
- fc2_weight_grad: float32 [3072, 768], P('dp', 'fsdp')
- fc2_bias_grad: float32 [768], P('fsdp')
Inputs may be any that keep to these rules, and one draw needn't show every extreme that they name: `latent_count`: exactly 8 slots hold no latent.
All inputs are finite; a program needn't handle non-finite values.
Results may differ from a plain program's by a relative error of at most 0.015.
The roundings to bfloat16 on the way count: a program that leaves them out, or rounds other values in their place, can miss the bound.
Values may be sent and summed in bfloat16 or wider, within the bound.
A program may use at most 128 MiB of HBM per device.

v0:
```python
import jax
import jax.numpy as jnp
from jax import lax
from jax.sharding import PartitionSpec as P

D = 768
HEADS = 12
HEAD = 64
FF = 3072


highest = lax.Precision.HIGHEST
bfloat = jnp.bfloat16


def normalize_rows(values):
    center = jnp.mean(values, axis=-1, keepdims=True)
    spread = jnp.mean(jnp.square(values - center), axis=-1, keepdims=True)
    inverse = lax.rsqrt(spread + 1e-06)
    return ((values - center) * inverse, inverse)


def norm_backward(grad_normed, normed, inverse):
    centered = grad_normed - jnp.mean(grad_normed, axis=-1, keepdims=True)
    return inverse * (centered - normed * jnp.mean(grad_normed * normed, axis=-1, keepdims=True))


def contract_rows(left_rows, right_rows):
    return lax.dot_general(
        left_rows, right_rows, (((0,), (0,)), ((), ())), preferred_element_type=jnp.float32
    )


def contract_exact(left_rows, right_rows):
    return lax.dot_general(left_rows, right_rows, (((0,), (0,)), ((), ())), precision=highest)


def against_weight(grad_rows, weight):
    return lax.dot_general(
        grad_rows, weight, (((1,), (1,)), ((), ())), preferred_element_type=jnp.float32
    )


def split_modulation(modulation):
    return jnp.split(modulation, 6, axis=-1)


def forward_local(latent_rows, cond_row, fullset):
    (
        ada_weight,
        qkv_weight,
        proj_weight,
        fc1_weight,
        fc2_weight,
        ada_bias,
        qv_bias,
        proj_bias,
        fc1_bias,
        fc2_bias,
    ) = fullset
    length = latent_rows.shape[0]
    rows_wide = latent_rows.astype(jnp.float32)
    cond_act = jax.nn.silu(cond_row.astype(jnp.float32)).astype(bfloat)
    modulation = jnp.dot(
        cond_act, ada_weight, preferred_element_type=jnp.float32
    ) + ada_bias.astype(jnp.float32)
    shift_one, scale_one, gate_one, shift_two, scale_two, gate_two = split_modulation(modulation)
    normed_one, inverse_one = normalize_rows(rows_wide)
    hidden_one = (normed_one * (1.0 + scale_one) + shift_one).astype(bfloat)
    qkv_bias = jnp.concatenate([qv_bias[:D], jnp.zeros((D,), bfloat), qv_bias[D:]]).astype(
        jnp.float32
    )
    projected = (
        jnp.dot(hidden_one, qkv_weight, preferred_element_type=jnp.float32) + qkv_bias
    ).astype(bfloat)
    queries = projected[:, :D].reshape(length, HEADS, HEAD)
    key_rows = projected[:, D : 2 * D].reshape(length, HEADS, HEAD)
    values = projected[:, 2 * D :].reshape(length, HEADS, HEAD)
    scores = jnp.einsum(
        "qhe,khe->hqk", queries, key_rows, preferred_element_type=jnp.float32
    ) * HEAD ** (-0.5)
    row_max = jnp.max(scores, axis=-1, keepdims=True)
    shifted = jnp.exp(scores - row_max)
    row_total = jnp.sum(shifted, axis=-1, keepdims=True)
    log_total = (row_max + jnp.log(row_total))[:, :, 0]
    probability = (shifted / row_total).astype(bfloat)
    attended = jnp.einsum("hqk,khe->qhe", probability, values, preferred_element_type=jnp.float32)
    attended = attended.reshape(length, D).astype(bfloat)
    branch = jnp.dot(attended, proj_weight, preferred_element_type=jnp.float32) + proj_bias.astype(
        jnp.float32
    )
    middle = rows_wide + gate_one * branch
    normed_two, inverse_two = normalize_rows(middle)
    hidden_two = (normed_two * (1.0 + scale_two) + shift_two).astype(bfloat)
    pre_gelu = jnp.dot(
        hidden_two, fc1_weight, preferred_element_type=jnp.float32
    ) + fc1_bias.astype(jnp.float32)
    activated = jax.nn.gelu(pre_gelu, approximate=True).astype(bfloat)
    mlp_out = jnp.dot(activated, fc2_weight, preferred_element_type=jnp.float32) + fc2_bias.astype(
        jnp.float32
    )
    block_out = (middle + gate_two * mlp_out).astype(bfloat)
    kept_state = (
        cond_act,
        modulation,
        normed_one,
        inverse_one,
        hidden_one,
        projected,
        log_total,
        attended,
        branch,
        normed_two,
        inverse_two,
        hidden_two,
        pre_gelu,
        activated,
        mlp_out,
    )
    return (block_out, kept_state)


def blank_forward(length):
    rows_f = jnp.zeros((length, D), jnp.float32)
    rows_b = jnp.zeros((length, D), bfloat)
    column_f = jnp.zeros((length, 1), jnp.float32)
    kept_state = (
        jnp.zeros((1, D), bfloat),
        jnp.zeros((1, 6 * D), jnp.float32),
        rows_f,
        column_f,
        rows_b,
        jnp.zeros((length, 3 * D), bfloat),
        jnp.zeros((HEADS, length), jnp.float32),
        rows_b,
        rows_f,
        rows_f,
        column_f,
        rows_b,
        jnp.zeros((length, FF), jnp.float32),
        jnp.zeros((length, FF), bfloat),
        rows_f,
    )
    return (rows_b, kept_state)


def backward_local(latent_rows, cond_row, cot_rows, kept_state, fullset):
    ada_weight, qkv_weight, proj_weight, fc1_weight, fc2_weight = fullset[:5]
    (
        cond_act,
        modulation,
        normed_one,
        inverse_one,
        hidden_one,
        projected,
        log_total,
        attended,
        branch,
        normed_two,
        inverse_two,
        hidden_two,
        pre_gelu,
        activated,
        mlp_out,
    ) = kept_state
    length = latent_rows.shape[0]
    shift_one, scale_one, gate_one, shift_two, scale_two, gate_two = split_modulation(modulation)
    grad_out = cot_rows.astype(jnp.float32)
    gate_two_grad = jnp.sum(grad_out * mlp_out, axis=0, keepdims=True)
    grad_mlp = (gate_two * grad_out).astype(bfloat)
    fc2_bias_grad = jnp.sum(grad_mlp.astype(jnp.float32), axis=0)
    grad_act = against_weight(grad_mlp, fc2_weight)
    gelu_pull = jax.vjp(lambda argument: jax.nn.gelu(argument, approximate=True), pre_gelu)[1]
    grad_pre = gelu_pull(grad_act)[0].astype(bfloat)
    fc1_bias_grad = jnp.sum(grad_pre.astype(jnp.float32), axis=0)
    grad_hidden_two = against_weight(grad_pre, fc1_weight)
    shift_two_grad = jnp.sum(grad_hidden_two, axis=0, keepdims=True)
    scale_two_grad = jnp.sum(grad_hidden_two * normed_two, axis=0, keepdims=True)
    grad_middle = grad_out + norm_backward(
        grad_hidden_two * (1.0 + scale_two), normed_two, inverse_two
    )
    gate_one_grad = jnp.sum(grad_middle * branch, axis=0, keepdims=True)
    grad_branch = (gate_one * grad_middle).astype(bfloat)
    proj_bias_grad = jnp.sum(grad_branch.astype(jnp.float32), axis=0)
    grad_attended = (
        against_weight(grad_branch, proj_weight).astype(bfloat).reshape(length, HEADS, HEAD)
    )
    queries = projected[:, :D].reshape(length, HEADS, HEAD)
    key_rows = projected[:, D : 2 * D].reshape(length, HEADS, HEAD)
    values = projected[:, 2 * D :].reshape(length, HEADS, HEAD)
    scale_factor = HEAD ** (-0.5)
    scores = (
        jnp.einsum("qhe,khe->hqk", queries, key_rows, preferred_element_type=jnp.float32)
        * scale_factor
    )
    probability = jnp.exp(scores - log_total[:, :, None])
    grad_prob = jnp.einsum(
        "qhe,khe->hqk", grad_attended, values, preferred_element_type=jnp.float32
    )
    inner_sum = jnp.sum(probability * grad_prob, axis=-1, keepdims=True)
    grad_scores = (probability * (grad_prob - inner_sum)).astype(bfloat)
    grad_queries = (
        jnp.einsum("hqk,khe->qhe", grad_scores, key_rows, preferred_element_type=jnp.float32)
        * scale_factor
    )
    grad_keys = (
        jnp.einsum("hqk,qhe->khe", grad_scores, queries, preferred_element_type=jnp.float32)
        * scale_factor
    )
    grad_values = jnp.einsum(
        "hqk,qhe->khe",
        probability.astype(bfloat),
        grad_attended,
        preferred_element_type=jnp.float32,
    )
    grad_projected = jnp.concatenate(
        [
            grad_queries.reshape(length, D),
            grad_keys.reshape(length, D),
            grad_values.reshape(length, D),
        ],
        axis=1,
    ).astype(bfloat)
    summed = jnp.sum(grad_projected.astype(jnp.float32), axis=0)
    qv_bias_grad = jnp.concatenate([summed[:D], summed[2 * D :]])
    grad_hidden_one = against_weight(grad_projected, qkv_weight)
    shift_one_grad = jnp.sum(grad_hidden_one, axis=0, keepdims=True)
    scale_one_grad = jnp.sum(grad_hidden_one * normed_one, axis=0, keepdims=True)
    latent_grad = (
        grad_middle + norm_backward(grad_hidden_one * (1.0 + scale_one), normed_one, inverse_one)
    ).astype(bfloat)
    mod_grad = jnp.concatenate(
        [
            shift_one_grad,
            scale_one_grad,
            gate_one_grad,
            shift_two_grad,
            scale_two_grad,
            gate_two_grad,
        ],
        axis=-1,
    )
    ada_bias_grad = mod_grad[0]
    cond_act_grad = lax.dot_general(
        mod_grad, ada_weight.astype(jnp.float32), (((1,), (1,)), ((), ())), precision=highest
    )
    cond_grad = jax.vjp(jax.nn.silu, cond_row.astype(jnp.float32))[1](cond_act_grad)[0]
    pairs = (
        hidden_one,
        attended,
        hidden_two,
        activated,
        grad_projected,
        grad_branch,
        grad_pre,
        grad_mlp,
    )
    return (
        latent_grad,
        cond_grad,
        pairs,
        (cond_act.astype(jnp.float32), mod_grad),
        (ada_bias_grad, qv_bias_grad, proj_bias_grad, fc1_bias_grad, fc2_bias_grad),
    )


def blank_backward(length):
    rows_b = jnp.zeros((length, D), bfloat)
    pairs = (
        rows_b,
        rows_b,
        rows_b,
        jnp.zeros((length, FF), bfloat),
        jnp.zeros((length, 3 * D), bfloat),
        rows_b,
        jnp.zeros((length, FF), bfloat),
        rows_b,
    )
    bias_zeros = (
        jnp.zeros((6 * D,), jnp.float32),
        jnp.zeros((2 * D,), jnp.float32),
        jnp.zeros((D,), jnp.float32),
        jnp.zeros((FF,), jnp.float32),
        jnp.zeros((D,), jnp.float32),
    )
    return (
        rows_b,
        jnp.zeros((1, D), jnp.float32),
        pairs,
        (jnp.zeros((1, D), jnp.float32), jnp.zeros((1, 6 * D), jnp.float32)),
        bias_zeros,
    )


def per_device(
    latents,
    conditioning,
    cotangent,
    latent_count,
    ada_weight,
    ada_bias,
    qkv_weight,
    qv_bias,
    proj_weight,
    proj_bias,
    fc1_weight,
    fc1_bias,
    fc2_weight,
    fc2_bias,
):
    has_latent = latent_count[0] > 0
    latent_rows = latents[0]
    cot_rows = cotangent[0]
    length = latent_rows.shape[0]
    column_full = (
        lax.all_gather(ada_weight, "fsdp", axis=1, tiled=True),
        lax.all_gather(qkv_weight, "fsdp", axis=1, tiled=True),
        lax.all_gather(proj_weight, "fsdp", axis=1, tiled=True),
        lax.all_gather(fc1_weight, "fsdp", axis=1, tiled=True),
        lax.all_gather(fc2_weight, "fsdp", axis=1, tiled=True),
        lax.all_gather(ada_bias, "fsdp", axis=0, tiled=True),
        lax.all_gather(qv_bias, "fsdp", axis=0, tiled=True),
        lax.all_gather(proj_bias, "fsdp", axis=0, tiled=True),
        lax.all_gather(fc1_bias, "fsdp", axis=0, tiled=True),
        lax.all_gather(fc2_bias, "fsdp", axis=0, tiled=True),
    )
    weights_full = (
        lax.all_gather(column_full[0], "dp", axis=0, tiled=True),
        lax.all_gather(column_full[1], "dp", axis=0, tiled=True),
        lax.all_gather(column_full[2], "dp", axis=0, tiled=True),
        lax.all_gather(column_full[3], "dp", axis=0, tiled=True),
        lax.all_gather(column_full[4], "dp", axis=0, tiled=True),
    )
    fullset = tuple(weights_full) + tuple(column_full[5:])
    block_out, kept_state = lax.cond(
        has_latent,
        lambda operands: forward_local(*operands),
        lambda operands: blank_forward(length),
        (latent_rows, conditioning, fullset),
    )
    column_back = (
        lax.all_gather(ada_weight, "fsdp", axis=1, tiled=True),
        lax.all_gather(qkv_weight, "fsdp", axis=1, tiled=True),
        lax.all_gather(proj_weight, "fsdp", axis=1, tiled=True),
        lax.all_gather(fc1_weight, "fsdp", axis=1, tiled=True),
        lax.all_gather(fc2_weight, "fsdp", axis=1, tiled=True),
        lax.all_gather(ada_bias, "fsdp", axis=0, tiled=True),
        lax.all_gather(qv_bias, "fsdp", axis=0, tiled=True),
        lax.all_gather(proj_bias, "fsdp", axis=0, tiled=True),
        lax.all_gather(fc1_bias, "fsdp", axis=0, tiled=True),
        lax.all_gather(fc2_bias, "fsdp", axis=0, tiled=True),
    )
    weights_back = (
        lax.all_gather(column_back[0], "dp", axis=0, tiled=True),
        lax.all_gather(column_back[1], "dp", axis=0, tiled=True),
        lax.all_gather(column_back[2], "dp", axis=0, tiled=True),
        lax.all_gather(column_back[3], "dp", axis=0, tiled=True),
        lax.all_gather(column_back[4], "dp", axis=0, tiled=True),
    )
    back_set = tuple(weights_back) + tuple(column_back[5:])
    latent_grad, cond_grad, pairs, ada_pair, bias_grads = lax.cond(
        has_latent,
        lambda operands: backward_local(*operands),
        lambda operands: blank_backward(length),
        (latent_rows, conditioning, cot_rows, kept_state, back_set),
    )
    column_index = lax.axis_index("fsdp")
    group_size = lax.axis_size("fsdp")
    cond_all, mod_all = (
        lax.all_gather(ada_pair[0], "fsdp", axis=0, tiled=True),
        lax.all_gather(ada_pair[1], "fsdp", axis=0, tiled=True),
    )
    mod_width = mod_all.shape[1] // group_size
    mod_owned = lax.dynamic_slice_in_dim(mod_all, column_index * mod_width, mod_width, 1)
    ada_local = contract_exact(cond_all, mod_owned)
    owned = (
        lax.all_to_all(pairs[4], "fsdp", split_axis=1, concat_axis=0, tiled=True),
        lax.all_to_all(pairs[5], "fsdp", split_axis=1, concat_axis=0, tiled=True),
        lax.all_to_all(pairs[6], "fsdp", split_axis=1, concat_axis=0, tiled=True),
        lax.all_to_all(pairs[7], "fsdp", split_axis=1, concat_axis=0, tiled=True),
    )
    initial = tuple(
        (
            jnp.zeros((pairs[index].shape[1], owned[index].shape[1]), jnp.float32)
            for index in range(4)
        )
    )
    pieces = (
        lax.all_gather(pairs[0], "fsdp", axis=0, tiled=True),
        lax.all_gather(pairs[1], "fsdp", axis=0, tiled=True),
        lax.all_gather(pairs[2], "fsdp", axis=0, tiled=True),
        lax.all_gather(pairs[3], "fsdp", axis=0, tiled=True),
    )
    folded = tuple(
        (contract_rows(pieces[index], owned[index]) for index, total in enumerate(initial))
    )
    weight_parts = (
        lax.psum_scatter(ada_local, "dp", scatter_dimension=0, tiled=True),
        lax.psum_scatter(folded[0], "dp", scatter_dimension=0, tiled=True),
        lax.psum_scatter(folded[1], "dp", scatter_dimension=0, tiled=True),
        lax.psum_scatter(folded[2], "dp", scatter_dimension=0, tiled=True),
        lax.psum_scatter(folded[3], "dp", scatter_dimension=0, tiled=True),
    )
    bias_columns = (
        lax.psum_scatter(bias_grads[0], "fsdp", scatter_dimension=0, tiled=True),
        lax.psum_scatter(bias_grads[1], "fsdp", scatter_dimension=0, tiled=True),
        lax.psum_scatter(bias_grads[2], "fsdp", scatter_dimension=0, tiled=True),
        lax.psum_scatter(bias_grads[3], "fsdp", scatter_dimension=0, tiled=True),
        lax.psum_scatter(bias_grads[4], "fsdp", scatter_dimension=0, tiled=True),
    )
    bias_parts = lax.psum(
        (bias_columns[0], bias_columns[1], bias_columns[2], bias_columns[3], bias_columns[4]), "dp"
    )
    return (
        block_out[None],
        latent_grad[None],
        cond_grad,
        weight_parts[0],
        bias_parts[0],
        weight_parts[1],
        bias_parts[1],
        weight_parts[2],
        bias_parts[2],
        weight_parts[3],
        bias_parts[3],
        weight_parts[4],
        bias_parts[4],
    )


def solution(mesh):
    in_specs = (
        P(("dp", "fsdp"), None, None),
        P(("dp", "fsdp"), None),
        P(("dp", "fsdp"), None, None),
        P(("dp", "fsdp")),
        P("dp", "fsdp"),
        P("fsdp"),
        P("dp", "fsdp"),
        P("fsdp"),
        P("dp", "fsdp"),
        P("fsdp"),
        P("dp", "fsdp"),
        P("fsdp"),
        P("dp", "fsdp"),
        P("fsdp"),
    )
    out_specs = (
        P(("dp", "fsdp"), None, None),
        P(("dp", "fsdp"), None, None),
        P(("dp", "fsdp"), None),
        P("dp", "fsdp"),
        P("fsdp"),
        P("dp", "fsdp"),
        P("fsdp"),
        P("dp", "fsdp"),
        P("fsdp"),
        P("dp", "fsdp"),
        P("fsdp"),
        P("dp", "fsdp"),
        P("fsdp"),
    )
    return jax.shard_map(
        per_device, mesh=mesh, in_specs=in_specs, out_specs=out_specs, check_vma=False
    )
```

profile of v0, /device:TPU:0, one launch (start us, length us, event | category | flops | bytes accessed | tf_op | source)
XLA Modules:
  0.0 923.0 jit_solution(13511667982497323485)
XLA Ops:
  7.2 0.7 all-gather.23.cloned.1.call-update
  8.0 0.7 all-gather.27.cloned.1.call-update
  8.7 0.7 all-gather.39.cloned.1.call-update
  9.4 0.9 copy.148
  10.3 16.6 %all_gather.79 = bf16[192,768]{0,1:T(8,128)(2,1)S(1)} all-gather(bf16[192,96]{0,1:T(8,128)(2,1)S(1)} %copy.148), channel_id=1, replica_groups=mesh['dp'=4,'fsdp'=8] {'fsdp'}, dimensions={1}, use_global_device_ids=true | all-gather | bytes 331776 | tf_op jit(solution)/shard_map/all_gather | solution.py:318
  26.9 0.9 copy.149
  27.8 1.0 copy.146
  28.9 18.0 %all_gather.76 = bf16[192,2304]{0,1:T(8,128)(2,1)S(1)} all-gather(bf16[192,288]{0,1:T(8,128)(2,1)S(1)} %copy.146), channel_id=1, replica_groups=mesh['dp'=4,'fsdp'=8] {'fsdp'}, dimensions={1}, use_global_device_ids=true | all-gather | bytes 995328 | tf_op jit(solution)/shard_map/all_gather | solution.py:317
  46.8 1.4 copy.147
  48.8 11.8 %all-gather.27.cloned.1.call-done = bf16[768,768]{0,1:T(8,128)(2,1)} async-done(((bf16[768,96]{0,1:T(8,128)(2,1)}), bf16[768,768]{0,1:T(8,128)(2,1)}) %all-gather.27.cloned.1.call-update) | async-done | bytes 1179664 | tf_op jit(solution)/shard_map/all_gather | solution.py:320
  60.7 29.4 %all-gather.39.cloned.1.call-done = bf16[8,576,192]{1,2,0:T(8,128)(2,1)} async-done(((bf16[1,576,192]{1,2,0:T(8,128)(2,1)}), bf16[8,576,192]{1,2,0:T(8,128)(2,1)}) %all-gather.39.cloned.1.call-update) | async-done | bytes 1769488 | tf_op jit(solution)/shard_map/all_gather | solution.py:316
  90.1 2.7 copy.145
  92.9 2.5 reshape.200
  98.7 12.7 %all-gather.1 = bf16[8,1,384]{2,1,0:T(2,128)(2,1)S(1)} all-gather(bf16[1,1,384]{2,1,0:T(2,128)(2,1)S(1)} %reshape.201), channel_id=1, replica_groups=mesh['dp'=4,'fsdp'=8] {'fsdp'}, dimensions={0}, use_global_device_ids=true | all-gather | bytes 6912 | tf_op jit(solution)/shard_map/all_gather | solution.py:324
  113.0 26.9 %all-reduce.11 = (bf16[4608]{0:T(1024)(128)(2,1)S(1)}, bf16[1536]{0:T(1024)(128)(2,1)S(1)}, bf16[768]{0:T(1024)(128)(2,1)}, bf16[768]{0:T(1024)(128)(2,1)}) all-reduce(bf16[4608]{0:T(1024)(128)(2,1)S(1)} %dynamic-update-slice, bf16[1536]{0:T(1024)(128)(2,1)S(1)} %dynamic-update-slice.1, ...), channel_id=1, replica_groups=mesh['dp'=4,'fsdp'=8] {'fsdp'}, use_global_device_ids=true, to_apply=%add | all-reduce | flops 7680 | bytes 30720
  139.9 28.7 %all-gather.19.cloned.1.call-done = bf16[768,2304]{1,0:T(8,128)(2,1)} async-done(((bf16[192,2304]{1,0:T(8,128)(2,1)}), bf16[768,2304]{1,0:T(8,128)(2,1)}) %all-gather.19.cloned.1.call-update) | async-done | bytes 3538960 | tf_op jit(solution)/shard_map/all_gather | solution.py:329
  168.7 58.8 %all-gather.25.cloned.1.call-done = bf16[768,3072]{1,0:T(8,128)(2,1)} async-done(((bf16[192,3072]{1,0:T(8,128)(2,1)}), bf16[768,3072]{1,0:T(8,128)(2,1)}) %all-gather.25.cloned.1.call-update) | async-done | bytes 4718608 | tf_op jit(solution)/shard_map/all_gather | solution.py:331
  227.4 59.0 %all-gather.29.cloned.1.call-done = bf16[3072,768]{0,1:T(8,128)(2,1)} async-done(((bf16[768,768]{0,1:T(8,128)(2,1)}), bf16[3072,768]{0,1:T(8,128)(2,1)}) %all-gather.29.cloned.1.call-update) | async-done | bytes 4718608 | tf_op jit(solution)/shard_map/all_gather | solution.py:332
  286.4 78.6 %all-gather.17.cloned.1.call-done = bf16[768,4608]{1,0:T(8,128)(2,1)} async-done(((bf16[192,4608]{1,0:T(8,128)(2,1)}), bf16[768,4608]{1,0:T(8,128)(2,1)}) %all-gather.17.cloned.1.call-update) | async-done | bytes 7077904 | tf_op jit(solution)/shard_map/all_gather | solution.py:328
  365.0 12.2 %conditional.2 = (bf16[1,768]{1,0:T(2,128)(2,1)S(1)}, f32[1,4608]{1,0:T(1,128)S(1)}, f32[256,768]{1,0:T(8,128)}, f32[256,1]{0,1:T(1,128)S(1)}, bf16[256,768]{1,0...) conditional(s32[]{:T(128)} %bitcast.25, () %tuple.30, ...), branch_computations={%region_0.0_spmd, %region_1.8_spmd} | conditional | flops 3856103936 | bytes 89583768 | solution.py:335
  365.0 1.0 broadcast.175
  366.0 0.8 broadcast.177
  366.7 1.1 broadcast.178
  367.9 0.8 broadcast.177.clone
  368.6 0.9 broadcast.175.clone
  369.6 0.9 broadcast.175.clone.1
  371.1 0.8 broadcast.177.clone.1
  371.8 2.1 broadcast.180
  373.9 1.3 broadcast.181
  375.2 0.9 broadcast.175.clone.2
  376.2 0.8 broadcast_in_dim.25
  377.2 10.3 %conditional.3 = (f32[1,768]{1,0:T(1,128)}, bf16[256,768]{1,0:T(8,128)(2,1)}, bf16[256,768]{1,0:T(8,128)(2,1)}, bf16[256,768]{1,0:T(8,128)(2,1)}, bf16[256,3072]...) conditional(s32[]{:T(128)} %bitcast.25, () %tuple.32, ...), branch_computations={%region_8.9_spmd, %region_9.25_spmd} | conditional | flops 4210357248 | bytes 154069600 | solution.py:361
  377.8 0.8 broadcast.190
  378.6 0.8 broadcast.190.clone
  379.4 0.8 broadcast.190.clone.1
  380.3 1.1 broadcast.192
  381.7 0.8 broadcast.190.clone.3
  386.6 0.8 broadcast_in_dim.27
  388.2 0.7 all-gather.35.cloned.1.call-update
  389.5 1.0 copy.155
  390.4 73.2 %all-to-all-start.1 = ((bf16[256,8,96]{0,2,1:T(8,128)(2,1)}), bf16[256,8,96]{0,2,1:T(8,128)(2,1)S(1)}, u32[]{:S(2)}, u32[]{:S(2)}) async-start(bf16[256,8,96]{0,2,1:T(8,128)(2,1)} %bitcast.36), calls=%async_computation.3 | async-start | bytes 786432 | tf_op jit(solution)/shard_map/all_to_all | solution.py:378
  463.6 29.5 %all-gather.2 = f32[8,1,768]{2,1,0:T(1,128)S(1)} all-gather(f32[1,1,768]{2,1,0:T(1,128)} %bitcast.32), channel_id=1, replica_groups=mesh['dp'=4,'fsdp'=8] {'fsdp'}, dimensions={0}, use_global_device_ids=true | all-gather | bytes 27648 | tf_op jit(solution)/shard_map/all_gather | solution.py:370
  493.2 14.5 %all-gather.3 = f32[8,1,4608]{2,1,0:T(1,128)S(1)} all-gather(f32[1,1,4608]{2,1,0:T(1,128)} %bitcast.33), channel_id=1, replica_groups=mesh['dp'=4,'fsdp'=8] {'fsdp'}, dimensions={0}, use_global_device_ids=true | all-gather | bytes 165888 | tf_op jit(solution)/shard_map/all_gather | solution.py:371
  507.8 3.1 fusion.51
  510.9 4.9 all-to-all-start
  515.8 1.6 copy.157
  517.4 48.4 %all-to-all-done = bf16[256,8,288]{0,2,1:T(8,128)(2,1)S(1)} async-done(((bf16[256,8,288]{0,2,1:T(8,128)(2,1)}), bf16[256,8,288]{0,2,1:T(8,128)(2,1)S(1)}, u32[]{:S(2)}, u32[]{:S(2)}) %all-to-all-start) | async-done | bytes 1179680 | tf_op jit(solution)/shard_map/all_to_all | solution.py:377
  565.7 3.6 all-to-all-start.2
  569.4 3.7 fusion.66
  573.2 1.2 copy.169
  574.4 5.2 fusion.65
  579.7 52.7 %all-to-all-done.2 = bf16[256,8,384]{0,2,1:T(8,128)(2,1)S(1)} async-done(((bf16[256,8,384]{0,2,1:T(8,128)(2,1)}), bf16[256,8,384]{0,2,1:T(8,128)(2,1)S(1)}, u32[]{:S(2)}, u32[]{:S(2)}) %all-to-all-start.2) | async-done | bytes 1572896 | tf_op jit(solution)/shard_map/all_to_all | solution.py:379
  632.4 0.9 copy.158
  633.2 4.7 fusion.67
  638.1 1.2 copy.159
  639.3 27.4 %all_to_all.76 = bf16[256,8,96]{0,2,1:T(8,128)(2,1)S(1)} all-to-all(bf16[256,8,96]{0,2,1:T(8,128)(2,1)S(1)} %bitcast.153), channel_id=1, replica_groups=mesh['dp'=4,'fsdp'=8] {'fsdp'}, dimensions={1} | all-to-all | bytes 786432 | tf_op jit(solution)/shard_map/all_to_all | solution.py:380
  666.7 90.5 %all-gather.37.cloned.1.call-done = bf16[2048,3072]{1,0:T(8,128)(2,1)} async-done(((bf16[256,3072]{1,0:T(8,128)(2,1)}), bf16[2048,3072]{1,0:T(8,128)(2,1)}) %all-gather.37.cloned.1.call-update) | async-done | bytes 12582928 | tf_op jit(solution)/shard_map/all_gather | solution.py:392
  757.1 7.8 fusion.68
  767.5 27.1 %all-reduce.9 = (f32[4608]{0:T(1024)S(1)}, f32[1536]{0:T(1024)S(1)}, f32[768]{0:T(1024)S(1)}, f32[3072]{0:T(1024)S(1)}, f32[768]{0:T(1024)S(1)}) all-reduce(f32[4608]{0:T(1024)} %get-tuple-element.172, f32[1536]{0:T(1024)} %get-tuple-element.175, f32[768]{0:T(1024)} %get-tuple-element.178, ...), channel_id=3, replica_groups=mesh['dp'=4,'fsdp'=8] {'fsdp'}, use_global_device_ids=true, to_apply=%region_26.27.clone | all-reduce | flops 10752 | bytes 86016
  795.0 10.8 %all-reduce.10 = (f32[576]{0:T(1024)}, f32[192]{0:T(256)}, f32[96]{0:T(128)}, f32[384]{0:T(512)}, f32[96]{0:T(128)}) all-reduce(f32[576]{0:T(1024)S(1)} %dynamic-slice.6, f32[192]{0:T(256)S(1)} %dynamic-slice.8, f32[96]{0:T(128)S(1)} %dynamic-slice.10, f32[384]{0:T(512)S(1)} %dynamic-slice.12, ...), channel_id=1, replica_groups=mesh['dp'=4,'fsdp'=8] {'dp'}, use_global_device_ids=true, to_apply=%region_27.28 | all-reduce | flops 1344 | bytes 10752 | tf_op jit(solution)/shard_map/psum | solution.py:411
  805.8 14.9 %reduce-scatter.10.cloned.1.call-done = f32[192,96]{1,0:T(8,128)} async-done(((f32[768,96]{1,0:T(8,128)}), f32[192,96]{1,0:T(8,128)}) %reduce-scatter.10.cloned.1.call-update) | async-done | bytes 73744 | tf_op jit(solution)/shard_map/reduce_scatter | solution.py:400
  820.7 31.9 %reduce-scatter.8.cloned.1.call-done = f32[192,288]{1,0:T(8,128)} async-done(((f32[768,288]{1,0:T(8,128)}), f32[192,288]{1,0:T(8,128)}) %reduce-scatter.8.cloned.1.call-update) | async-done | bytes 221200 | tf_op jit(solution)/shard_map/reduce_scatter | solution.py:399
  852.7 31.9 %reduce-scatter.12.cloned.1.call-done = f32[192,384]{1,0:T(8,128)} async-done(((f32[768,384]{1,0:T(8,128)}), f32[192,384]{1,0:T(8,128)}) %reduce-scatter.12.cloned.1.call-update) | async-done | bytes 294928 | tf_op jit(solution)/shard_map/reduce_scatter | solution.py:401
  884.6 31.9 %reduce-scatter.14.cloned.1.call-done = f32[768,96]{0,1:T(8,128)} async-done(((f32[3072,96]{0,1:T(8,128)}), f32[768,96]{0,1:T(8,128)}) %reduce-scatter.14.cloned.1.call-update) | async-done | bytes 294928 | tf_op jit(solution)/shard_map/reduce_scatter | solution.py:402
  (91 shorter events, 10.9 us)
Async XLA Ops:
  7.2 41.1 %all-gather.23.cloned.1.call-start = ((), (), s32[]{:S(2)}) async-start(), calls=%async_computation.12 | async-start | bytes 1327104 | tf_op jit(solution)/shard_map/all_gather | solution.py:319
  7.9 52.7 %all-gather.27.cloned.1.call-start = ((), (), s32[]{:S(2)}) async-start(), calls=%async_computation.14 | async-start | bytes 1327104 | tf_op jit(solution)/shard_map/all_gather | solution.py:320
  8.7 81.5 %all-gather.39.cloned.1.call-start = ((), (), s32[]{:S(2)}) async-start(), calls=%async_computation.25 | async-start | bytes 2211840 | tf_op jit(solution)/shard_map/all_gather | solution.py:316
  9.4 130.5 %all-gather.21.cloned.1.call-start = ((), (), s32[]{:S(2)}) async-start(), calls=%async_computation.11 | async-start | bytes 1474560 | tf_op jit(solution)/shard_map/all_gather | solution.py:330
  27.8 140.9 %all-gather.19.cloned.1.call-start = ((), (), s32[]{:S(2)}) async-start(), calls=%async_computation.10 | async-start | bytes 4423680 | tf_op jit(solution)/shard_map/all_gather | solution.py:329
  48.2 179.2 %all-gather.25.cloned.1.call-start = ((), (), s32[]{:S(2)}) async-start(), calls=%async_computation.13 | async-start | bytes 5898240 | tf_op jit(solution)/shard_map/all_gather | solution.py:331
  48.8 237.6 %all-gather.29.cloned.1.call-start = ((), (), s32[]{:S(2)}) async-start(), calls=%async_computation.15 | async-start | bytes 5898240 | tf_op jit(solution)/shard_map/all_gather | solution.py:332
  60.7 304.3 %all-gather.17.cloned.1.call-start = ((), (), s32[]{:S(2)}) async-start(), calls=%async_computation.9 | async-start | bytes 8847360 | tf_op jit(solution)/shard_map/all_gather | solution.py:328
  92.8 3.4 copy-start.30
  92.8 5.9 copy-start.32
  92.8 19.3 %copy-start.35 = (bf16[96]{0:T(256)(128)(2,1)S(1)}, bf16[96]{0:T(256)(128)(2,1)}, u32[]{:S(2)}) copy-start(bf16[96]{0:T(256)(128)(2,1)} %param.27) | copy-start | bytes 580
  92.8 19.4 %copy-start.36 = (bf16[96]{0:T(256)(128)(2,1)S(1)}, bf16[96]{0:T(256)(128)(2,1)}, u32[]{:S(2)}) copy-start(bf16[96]{0:T(256)(128)(2,1)} %param.31) | copy-start | bytes 580
  92.8 19.7 %copy-start.31 = (bf16[576]{0:T(1024)(128)(2,1)S(1)}, bf16[576]{0:T(1024)(128)(2,1)}, u32[]{:S(2)}) copy-start(bf16[576]{0:T(1024)(128)(2,1)} %param.23) | copy-start | bytes 3460
  92.9 19.9 %copy-start.37 = (bf16[192]{0:T(256)(128)(2,1)S(1)}, bf16[192]{0:T(256)(128)(2,1)}, u32[]{:S(2)}) copy-start(bf16[192]{0:T(256)(128)(2,1)} %param.25) | copy-start | bytes 1156
  92.9 272.1 %copy-start = (bf16[1,256,768]{2,1,0:T(8,128)(2,1)S(1)}, bf16[1,256,768]{2,1,0:T(8,128)(2,1)}, u32[]{:S(2)}) copy-start(bf16[1,256,768]{2,1,0:T(8,128)(2,1)} %param.18) | copy-start | bytes 1179652
  92.9 272.1 %copy-start.22 = (bf16[1,768]{1,0:T(2,128)(2,1)S(1)}, bf16[1,768]{1,0:T(2,128)(2,1)}, u32[]{:S(2)}) copy-start(bf16[1,768]{1,0:T(2,128)(2,1)} %param.19) | copy-start | bytes 4612
  95.4 474.0 %all-gather.33.cloned.1.call-start = ((), (), s32[]{:S(2)}) async-start(), calls=%async_computation.19 | async-start | bytes 3538944 | tf_op jit(solution)/shard_map/all_gather | solution.py:390
  387.5 1.4 copy-start.1
  387.6 186.8 %all-gather.31.cloned.1.call-start = ((), (), s32[]{:S(2)}) async-start(), calls=%async_computation.17 | async-start | bytes 3538944 | tf_op jit(solution)/shard_map/all_gather | solution.py:389
  388.1 245.1 %all-gather.35.cloned.1.call-start = ((), (), s32[]{:S(2)}) async-start(), calls=%async_computation.21 | async-start | bytes 3538944 | tf_op jit(solution)/shard_map/all_gather | solution.py:391
  388.9 368.3 %all-gather.37.cloned.1.call-start = ((), (), s32[]{:S(2)}) async-start(), calls=%async_computation.23 | async-start | bytes 14155776 | tf_op jit(solution)/shard_map/all_gather | solution.py:392
  390.4 120.4 %all-to-all-start.1 = ((bf16[256,8,96]{0,2,1:T(8,128)(2,1)}), bf16[256,8,96]{0,2,1:T(8,128)(2,1)S(1)}, u32[]{:S(2)}, u32[]{:S(2)}) async-start(bf16[256,8,96]{0,2,1:T(8,128)(2,1)} %bitcast.36), calls=%async_computation.3 | async-start | bytes 786432 | tf_op jit(solution)/shard_map/all_to_all | solution.py:378
  463.6 342.2 %reduce-scatter.6.cloned.1.call-start = ((), (), s32[]{:S(2)}) async-start(), calls=%async_computation.16 | async-start | bytes 2457600 | tf_op jit(solution)/shard_map/reduce_scatter | solution.py:398
  510.9 54.9 %all-to-all-start = ((bf16[256,8,288]{0,2,1:T(8,128)(2,1)}), bf16[256,8,288]{0,2,1:T(8,128)(2,1)S(1)}, u32[]{:S(2)}, u32[]{:S(2)}) async-start(bf16[256,8,288]{0,2,1:T(8,128)(2,1)} %bitcast.34), calls=%async_computation.1 | async-start | bytes 2359296 | tf_op jit(solution)/shard_map/all_to_all | solution.py:377
  565.7 66.6 %all-to-all-start.2 = ((bf16[256,8,384]{0,2,1:T(8,128)(2,1)}), bf16[256,8,384]{0,2,1:T(8,128)(2,1)S(1)}, u32[]{:S(2)}, u32[]{:S(2)}) async-start(bf16[256,8,384]{0,2,1:T(8,128)(2,1)} %bitcast.38), calls=%async_computation.5 | async-start | bytes 3145728 | tf_op jit(solution)/shard_map/all_to_all | solution.py:379
  569.3 251.4 %reduce-scatter.10.cloned.1.call-start = ((), (), s32[]{:S(2)}) async-start(), calls=%async_computation.20 | async-start | bytes 491520 | tf_op jit(solution)/shard_map/reduce_scatter | solution.py:400
  573.1 279.5 %reduce-scatter.8.cloned.1.call-start = ((), (), s32[]{:S(2)}) async-start(), calls=%async_computation.18 | async-start | bytes 1474560 | tf_op jit(solution)/shard_map/reduce_scatter | solution.py:399
  579.6 305.0 %reduce-scatter.12.cloned.1.call-start = ((), (), s32[]{:S(2)}) async-start(), calls=%async_computation.22 | async-start | bytes 1474560 | tf_op jit(solution)/shard_map/reduce_scatter | solution.py:401
  638.0 278.5 %reduce-scatter.14.cloned.1.call-start = ((), (), s32[]{:S(2)}) async-start(), calls=%async_computation.24 | async-start | bytes 1474560 | tf_op jit(solution)/shard_map/reduce_scatter | solution.py:402
Sparse Core Ops, SparseCore 0:
  9.6 27.4 all-gather.22
  38.8 21.8 all-gather.26
  62.3 27.7 all-gather.38
  92.4 27.2 all-gather.20
  121.4 47.2 all-gather.18
  170.3 57.0 all-gather.24
  229.3 57.0 all-gather.28
  288.2 76.6 all-gather.16
  387.7 116.2 all-gather.32
  505.5 59.2 all-gather.30
  566.4 65.9 all-gather.34
  633.9 123.2 all-gather.36
  760.8 32.2 reduce-scatter.5
  796.3 24.3 reduce-scatter.9
  824.1 28.5 reduce-scatter.7
  856.0 28.5 reduce-scatter.11
  887.9 28.5 reduce-scatter.13
where the time goes:
time: 930 us; the launch traced here: 923 us
  waiting for transfers between devices  573 us (62%)
  blocking collectives  183 us (20%)
  starting transfers between devices  82.3 us (9%)
  local copies, waits for them, and re-layouts  39.9 us (4%)
  matrix products  24.5 us (3%)
  between operations  19.4 us (2%)
    all_gather x1, waiting for transfers between devices, per_device(): lax.all_gather(pairs[3], 'fsdp', axis=0, tiled=True)  90.5 us
    all_gather x1, waiting for transfers between devices, per_device(): lax.all_gather(column_full[0], 'dp', axis=0, tiled=True)  78.6 us
    all_to_all x1, starting transfers between devices, per_device(): lax.all_to_all(pairs[5], 'fsdp', split_axis=1, concat_axis=0, tiled=True)  73.2 us
    all_gather x1, waiting for transfers between devices, per_device(): lax.all_gather(column_full[4], 'dp', axis=0, tiled=True)  59 us
    all_gather x1, waiting for transfers between devices, per_device(): lax.all_gather(column_full[3], 'dp', axis=0, tiled=True)  58.8 us
    unnamed x2, blocking collectives  54 us
    all_to_all x1, waiting for transfers between devices, per_device(): lax.all_to_all(pairs[6], 'fsdp', split_axis=1, concat_axis=0, tiled=True)  52.7 us
    all_to_all x1, waiting for transfers between devices, per_device(): lax.all_to_all(pairs[4], 'fsdp', split_axis=1, concat_axis=0, tiled=True)  48.4 us
  transfers between devices with their start and end apart: 20, of which 13 were waited for; matrix products, arithmetic and copies ran while one was open for 5% of the time, Pallas kernels for 0%

commit v1 on v0

v1 whole, which is shorter than its diff:
```python
import functools
import jax
import jax.numpy as jnp
from jax import lax
from jax.sharding import PartitionSpec as P
from jax.experimental import pallas as pl
from jax.experimental.pallas import tpu as pltpu

MESH_IDS = pl.DeviceIdType.MESH
D = 768
HEADS = 12
HEAD = 64
FF = 3072

highest = lax.Precision.HIGHEST
bfloat = jnp.bfloat16


def place(dp_index, z_index, core):
    return (dp_index, z_index * 2 + core)


def z_order(size):
    steps = [0]
    for distance in range(1, size // 2 + 1):
        steps.append(distance)
        if size - distance != distance:
            steps.append(size - distance)
    return steps


def enter_barrier(partners):
    barrier = pltpu.get_barrier_semaphore()
    for partner in partners:
        pl.semaphore_signal(barrier, inc=1, device_id=partner, device_id_type=MESH_IDS)
    pl.semaphore_wait(barrier, len(partners))


def positions(rows, depth):
    dp = lax.axis_index("dp")
    column = lax.axis_index("fsdp")
    z, core = column // 2, column % 2
    others = [(dp ^ 1), (dp ^ 2)] if rows == 4 else [(dp + step) % rows for step in range(1, rows)]
    partners = [place(dp, z, 1 - core)]
    partners += [place(other, z, core) for other in others]
    partners += [place(dp, (z + step) % depth, core) for step in z_order(depth)[1:]]
    return dp, z, core, others, partners


def gather_kernel(rows, depth, shard, out, own_sem, send_sems, recv_sems):
    dp, z, core, others, partners = positions(rows, depth)
    height = shard.shape[0]
    half = height // 2
    sibling = place(dp, z, 1 - core)
    enter_barrier(partners)
    sends = []

    def send(source, line, row, part, target):
        destination, origin = out.at[line, row], source
        if part is not None and rows == 4:
            if part[1]:
                destination = destination.at[pl.ds(part[0] * half, half)]
                origin = source.at[pl.ds(part[0] * half, half)]
        slot = part[0] if part is not None else 0
        copy = pltpu.make_async_remote_copy(
            src_ref=origin,
            dst_ref=destination,
            send_sem=send_sems.at[len(sends)],
            recv_sem=recv_sems.at[slot, line, row],
            device_id=target,
            device_id_type=MESH_IDS,
        )
        copy.start()
        sends.append(copy)

    def arrive(line, row, part=None):
        destination = out.at[line, row]
        slot = 0
        if part is not None:
            slot = part
            destination = destination.at[pl.ds(part * half, half)]
        pltpu.make_async_remote_copy(
            src_ref=destination,
            dst_ref=destination,
            send_sem=send_sems.at[0],
            recv_sem=recv_sems.at[slot, line, row],
            device_id=sibling,
            device_id_type=MESH_IDS,
        ).wait_recv()

    own = z * 2 + core
    steps = z_order(depth)
    lines = [((z - step) % depth) * 2 + core for step in steps]
    for other in others:
        send(shard, own, dp, None, place(other, z, core))
    for step in steps[1:]:
        send(shard, own, dp, None, place(dp, (z + step) % depth, core))
    send(shard, own, dp, None, sibling)
    keep = pltpu.make_async_copy(shard, out.at[own, dp], own_sem)
    keep.start()
    for turn in range(depth + 2):
        if 0 < turn < depth:
            line = lines[turn]
            arrive(line, dp)
            for other in others:
                send(out.at[line, dp], line, dp, None, place(other, z, core))
            send(out.at[line, dp], line, dp, None, sibling)
        if 1 <= turn <= depth:
            line = lines[turn - 1]
            for position, other in enumerate(others):
                arrive(line, other)
                if rows == 4:
                    send(out.at[line, other], line, other, (position, True), place(others[1 - position], z, core))
                send(out.at[line, other], line, other, None, sibling)
        if turn >= 2 and rows == 4:
            line = lines[turn - 2]
            arrive(line, dp ^ 3, 0)
            arrive(line, dp ^ 3, 1)
            send(out.at[line, dp ^ 3], line, dp ^ 3, None, sibling)
    for line in lines:
        for row in range(rows):
            arrive(line + 1 - 2 * core, (dp + row) % rows)
    keep.wait()
    for copy in sends:
        copy.wait_send()


def gather_shards(shard, rows, columns):
    depth = columns // 2
    count = (depth - 1) + depth * rows + depth * (rows - 1) + (2 * depth if rows == 4 else 0)
    return pl.pallas_call(
        functools.partial(gather_kernel, rows, depth),
        out_shape=jax.ShapeDtypeStruct((columns, rows) + shard.shape, shard.dtype),
        in_specs=[pl.BlockSpec(memory_space=pl.ANY)],
        out_specs=pl.BlockSpec(memory_space=pl.ANY),
        scratch_shapes=[
            pltpu.SemaphoreType.DMA,
            pltpu.SemaphoreType.DMA((count,)),
            pltpu.SemaphoreType.DMA((2, columns, rows)),
        ],
        compiler_params=pltpu.CompilerParams(collective_id=0, has_side_effects=True),
        name="gather_shards",
    )(shard)


def scatter_kernel(
    rows, depth, grads, out, held, pair, plane, cross, along,
    load_sems, pair_send, pair_recv, plane_send, plane_recv, cross_send, cross_recv, along_send, along_recv,
):
    dp, z, core, others, partners = positions(rows, depth)
    height = out.shape[0]
    half = height // 2
    chunk = 48
    sibling = place(dp, z, 1 - core)
    targets = [dp ^ 3, dp ^ 1, dp ^ 2, dp] if rows == 4 else others + [dp]
    steps = z_order(depth)[::-1]
    enter_barrier(partners)
    waits = []

    def remote(source, destination, send_sem, recv_sem, target):
        return pltpu.make_async_remote_copy(
            src_ref=source, dst_ref=destination, send_sem=send_sem, recv_sem=recv_sem,
            device_id=target, device_id_type=MESH_IDS,
        )

    def start(copy):
        copy.start()
        waits.append(copy)
        return copy

    def add(first, others_in, length, target):
        @pl.loop(0, length // chunk)
        def _(index):
            piece = pl.ds(pl.multiple_of(index * chunk, chunk), chunk)
            total = first[piece, :].astype(jnp.float32)
            for other in others_in:
                total = total + other[piece, :].astype(jnp.float32)
            target[piece, :] = total.astype(target.dtype)

    lines = [(z + step) % depth for step in steps]
    pairs, loads = {}, {}
    for turn, line in enumerate(lines):
        for slot, target in enumerate(targets):
            pairs[turn, slot] = start(remote(
                grads.at[line * 2 + 1 - core, target], pair.at[turn, slot],
                pair_send.at[turn, slot], pair_recv.at[turn, slot], sibling))
            loads[turn, slot] = pltpu.make_async_copy(
                grads.at[line * 2 + core, target], held.at[turn, slot], load_sems.at[turn, slot])
            loads[turn, slot].start()
    last = len(targets) - 1
    planes, crosses, alongs = {}, {}, {}
    for turn in range(depth + 2):
        if turn < depth:
            for slot in range(len(targets)):
                loads[turn, slot].wait()
                pairs[turn, slot].wait_recv()
                here = held.at[turn, slot]
                add(here, [pair.at[turn, slot]], height, here)
                if rows == 4 and slot == 0:
                    for position in range(2):
                        part = pl.ds((1 - position) * half, half)
                        crosses[turn, position] = start(remote(
                            held.at[turn, 0, part], cross.at[turn, position],
                            cross_send.at[turn, position], cross_recv.at[turn, position],
                            place(others[position], z, core)))
                if rows != 4 and slot < last:
                    planes[turn, slot] = start(remote(
                        here, plane.at[turn, slot], plane_send.at[turn, slot],
                        plane_recv.at[turn, slot], place(targets[slot], z, core)))
        if rows == 4 and 1 <= turn <= depth:
            now = turn - 1
            for position in range(2):
                crosses[now, 1 - position].wait_recv()
                part = held.at[now, 1 + position, pl.ds(position * half, half)]
                add(part, [cross.at[now, 1 - position]], half, part)
                planes[now, position] = start(remote(
                    held.at[now, 1 + position], plane.at[now, position],
                    plane_send.at[now, position], plane_recv.at[now, position],
                    place(others[position], z, core)))
        if turn >= 2:
            now = turn - 2
            for slot in range(len(others)):
                planes[now, slot].wait_recv()
            here = held.at[now, last]
            add(here, [plane.at[now, slot] for slot in range(len(others))], height, here)
            if now < depth - 1:
                alongs[now] = start(remote(
                    here, along.at[now], along_send.at[now], along_recv.at[now],
                    place(dp, lines[now], core)))
    for now in range(depth - 1):
        alongs[now].wait_recv()
    add(held.at[depth - 1, last], [along.at[now] for now in range(depth - 1)], height, out)
    for copy in waits:
        copy.wait_send()


def scatter_shards(grads):
    columns, rows, height, width = grads.shape
    depth = columns // 2
    peers = 2 if rows == 4 else rows - 1
    half = height // 2 if rows == 4 else 16
    dma = pltpu.SemaphoreType.DMA
    kind = grads.dtype
    return pl.pallas_call(
        functools.partial(scatter_kernel, rows, depth),
        out_shape=jax.ShapeDtypeStruct((height, width), jnp.float32),
        in_specs=[pl.BlockSpec(memory_space=pl.ANY)],
        out_specs=pl.BlockSpec(memory_space=pltpu.VMEM),
        scratch_shapes=[
            pltpu.VMEM((depth, rows, height, width), kind),
            pltpu.VMEM((depth, rows, height, width), kind),
            pltpu.VMEM((depth, peers, height, width), kind),
            pltpu.VMEM((depth, 2, half, width), kind),
            pltpu.VMEM((depth - 1, height, width), kind),
            dma((depth, rows)), dma((depth, rows)), dma((depth, rows)),
            dma((depth, peers)), dma((depth, peers)),
            dma((depth, 2)), dma((depth, 2)),
            dma((depth - 1,)), dma((depth - 1,)),
        ],
        compiler_params=pltpu.CompilerParams(
            collective_id=1, has_side_effects=True, vmem_limit_bytes=50 * 2**20),
        name="scatter_shards",
    )(grads)


def normalize_rows(values):
    center = jnp.mean(values, axis=-1, keepdims=True)
    spread = jnp.mean(jnp.square(values - center), axis=-1, keepdims=True)
    inverse = lax.rsqrt(spread + 1e-06)
    return ((values - center) * inverse, inverse)


def norm_backward(grad_normed, normed, inverse):
    centered = grad_normed - jnp.mean(grad_normed, axis=-1, keepdims=True)
    return inverse * (centered - normed * jnp.mean(grad_normed * normed, axis=-1, keepdims=True))


def contract_rows(left_rows, right_rows):
    return lax.dot_general(
        left_rows, right_rows, (((0,), (0,)), ((), ())), preferred_element_type=jnp.float32
    )


def contract_exact(left_rows, right_rows):
    return lax.dot_general(left_rows, right_rows, (((0,), (0,)), ((), ())), precision=highest)


def against_weight(grad_rows, weight):
    return lax.dot_general(
        grad_rows, weight, (((1,), (1,)), ((), ())), preferred_element_type=jnp.float32
    )


def layer(latent_rows, cond_act, live, cot_rows, modulation, weights, biases):
    qkv_weight, proj_weight, fc1_weight, fc2_weight = weights
    qv_bias, proj_bias, fc1_bias, fc2_bias = biases
    length = latent_rows.shape[0]
    rows_wide = latent_rows.astype(jnp.float32)
    shift_one, scale_one, gate_one, shift_two, scale_two, gate_two = jnp.split(
        modulation, 6, axis=-1
    )
    normed_one, inverse_one = normalize_rows(rows_wide)
    hidden_one = (normed_one * (1.0 + scale_one) + shift_one).astype(bfloat)
    qkv_bias = jnp.concatenate([qv_bias[:D], jnp.zeros((D,), jnp.float32), qv_bias[D:]])
    projected = (
        jnp.dot(hidden_one, qkv_weight, preferred_element_type=jnp.float32) + qkv_bias
    ).astype(bfloat)
    queries = projected[:, :D].reshape(length, HEADS, HEAD)
    key_rows = projected[:, D : 2 * D].reshape(length, HEADS, HEAD)
    values = projected[:, 2 * D :].reshape(length, HEADS, HEAD)
    scale_factor = HEAD ** (-0.5)
    scores = (
        jnp.einsum("qhe,khe->hqk", queries, key_rows, preferred_element_type=jnp.float32)
        * scale_factor
    )
    row_max = jnp.max(scores, axis=-1, keepdims=True)
    shifted = jnp.exp(scores - row_max)
    row_total = jnp.sum(shifted, axis=-1, keepdims=True)
    exact_probability = shifted / row_total
    probability = exact_probability.astype(bfloat)
    attended = jnp.einsum("hqk,khe->qhe", probability, values, preferred_element_type=jnp.float32)
    attended = attended.reshape(length, D).astype(bfloat)
    branch = jnp.dot(attended, proj_weight, preferred_element_type=jnp.float32) + proj_bias
    middle = rows_wide + gate_one * branch
    normed_two, inverse_two = normalize_rows(middle)
    hidden_two = (normed_two * (1.0 + scale_two) + shift_two).astype(bfloat)
    pre_gelu = jnp.dot(hidden_two, fc1_weight, preferred_element_type=jnp.float32) + fc1_bias
    activated, gelu_pull = jax.vjp(
        lambda argument: jax.nn.gelu(argument, approximate=True), pre_gelu
    )
    activated = activated.astype(bfloat)
    mlp_out = jnp.dot(activated, fc2_weight, preferred_element_type=jnp.float32) + fc2_bias
    block_out = (live * (middle + gate_two * mlp_out)).astype(bfloat)

    grad_out = live * cot_rows.astype(jnp.float32)
    gate_two_grad = jnp.sum(grad_out * mlp_out, axis=0, keepdims=True)
    grad_mlp = (gate_two * grad_out).astype(bfloat)
    fc2_bias_grad = jnp.sum(grad_mlp.astype(jnp.float32), axis=0)
    grad_act = against_weight(grad_mlp, fc2_weight)
    grad_pre = gelu_pull(grad_act)[0].astype(bfloat)
    fc1_bias_grad = jnp.sum(grad_pre.astype(jnp.float32), axis=0)
    grad_hidden_two = against_weight(grad_pre, fc1_weight)
    shift_two_grad = jnp.sum(grad_hidden_two, axis=0, keepdims=True)
    scale_two_grad = jnp.sum(grad_hidden_two * normed_two, axis=0, keepdims=True)
    grad_middle = grad_out + norm_backward(
        grad_hidden_two * (1.0 + scale_two), normed_two, inverse_two
    )
    gate_one_grad = jnp.sum(grad_middle * branch, axis=0, keepdims=True)
    grad_branch = (gate_one * grad_middle).astype(bfloat)
    proj_bias_grad = jnp.sum(grad_branch.astype(jnp.float32), axis=0)
    grad_attended = (
        against_weight(grad_branch, proj_weight).astype(bfloat).reshape(length, HEADS, HEAD)
    )
    grad_prob = jnp.einsum(
        "qhe,khe->hqk", grad_attended, values, preferred_element_type=jnp.float32
    )
    inner_sum = jnp.sum(exact_probability * grad_prob, axis=-1, keepdims=True)
    grad_scores = (exact_probability * (grad_prob - inner_sum)).astype(bfloat)
    grad_queries = (
        jnp.einsum("hqk,khe->qhe", grad_scores, key_rows, preferred_element_type=jnp.float32)
        * scale_factor
    )
    grad_keys = (
        jnp.einsum("hqk,qhe->khe", grad_scores, queries, preferred_element_type=jnp.float32)
        * scale_factor
    )
    grad_values = jnp.einsum(
        "hqk,qhe->khe", probability, grad_attended, preferred_element_type=jnp.float32
    )
    grad_projected = jnp.concatenate(
        [
            grad_queries.reshape(length, D),
            grad_keys.reshape(length, D),
            grad_values.reshape(length, D),
        ],
        axis=1,
    ).astype(bfloat)
    summed = jnp.sum(grad_projected.astype(jnp.float32), axis=0)
    qv_bias_grad = jnp.concatenate([summed[:D], summed[2 * D :]])
    grad_hidden_one = against_weight(grad_projected, qkv_weight)
    shift_one_grad = jnp.sum(grad_hidden_one, axis=0, keepdims=True)
    scale_one_grad = jnp.sum(grad_hidden_one * normed_one, axis=0, keepdims=True)
    latent_grad = (
        grad_middle + norm_backward(grad_hidden_one * (1.0 + scale_one), normed_one, inverse_one)
    ).astype(bfloat)
    mod_grad = jnp.concatenate(
        [
            shift_one_grad,
            scale_one_grad,
            gate_one_grad,
            shift_two_grad,
            scale_two_grad,
            gate_two_grad,
        ],
        axis=-1,
    )
    weight_grads = (
        contract_rows(hidden_one, grad_projected).astype(bfloat),
        contract_rows(attended, grad_branch).astype(bfloat),
        contract_rows(hidden_two, grad_pre).astype(bfloat),
        contract_rows(activated, grad_mlp).astype(bfloat),
    )
    bias_grads = (qv_bias_grad, proj_bias_grad, fc1_bias_grad, fc2_bias_grad)
    return block_out, latent_grad, mod_grad, weight_grads, bias_grads


def pack_shard(qkv, proj, fc1, fc2):
    tall = fc2.shape[0] // fc1.shape[0]
    folded = fc2.reshape(tall, fc1.shape[0], fc2.shape[1]).transpose(1, 0, 2).reshape(fc1.shape)
    return jnp.concatenate([jnp.concatenate([qkv, proj], axis=1), fc1, folded], axis=0)


def unpack_shard(shard, qkv_width, low_width):
    height = shard.shape[0] // 3
    tall = shard.shape[1] // low_width
    first, second, third = shard[:height], shard[height : 2 * height], shard[2 * height :]
    folded = third.reshape(height, tall, low_width).transpose(1, 0, 2).reshape(-1, low_width)
    return first[:, :qkv_width], first[:, qkv_width:], second, folded


def unpack_full(blocks, qkv_width, low_width):
    columns, rows, height, width = blocks.shape
    height = height // 3
    tall = width // low_width

    def wide(part):
        return part.transpose(1, 2, 0, 3).reshape(rows * height, -1)

    first = blocks[:, :, :height]
    fc2 = blocks[:, :, 2 * height :].reshape(columns, rows, height, tall, low_width)
    return (
        wide(first[..., :qkv_width]),
        wide(first[..., qkv_width:]),
        wide(blocks[:, :, height : 2 * height]),
        fc2.transpose(1, 3, 2, 0, 4).reshape(rows * tall * height, columns * low_width),
    )


def pack_full(weight_grads, columns, rows):
    qkv, proj, fc1, fc2 = weight_grads
    height = qkv.shape[0] // rows

    def blocked(grad):
        return grad.reshape(rows, height, columns, -1).transpose(2, 0, 1, 3)

    tall = fc2.shape[0] // (rows * height)
    folded = fc2.reshape(rows, tall, height, columns, -1).transpose(3, 0, 2, 1, 4)
    folded = folded.reshape(columns, rows, height, -1)
    first = jnp.concatenate([blocked(qkv), blocked(proj)], axis=3)
    return jnp.concatenate([first, blocked(fc1), folded], axis=2)


def per_device(
    latents,
    conditioning,
    cotangent,
    latent_count,
    ada_weight,
    ada_bias,
    qkv_weight,
    qv_bias,
    proj_weight,
    proj_bias,
    fc1_weight,
    fc1_bias,
    fc2_weight,
    fc2_bias,
):
    rows, columns = lax.axis_size("dp"), lax.axis_size("fsdp")
    row_index = lax.axis_index("dp")
    live = latent_count[0].astype(jnp.float32)
    depth = ada_weight.shape[0]
    mod_width = ada_weight.shape[1]
    own_biases = (qv_bias, proj_bias, fc1_bias, fc2_bias)
    widths = [bias.shape[0] for bias in own_biases]
    cuts = [mod_width + sum(widths[:place]) for place in range(len(widths))]

    cond_row = conditioning.astype(jnp.float32)
    cond_act = jax.nn.silu(cond_row).astype(bfloat)
    cond_all = lax.all_gather(cond_act, ("dp", "fsdp"), axis=0, tiled=True)
    cond_owned = lax.dynamic_slice_in_dim(cond_all, row_index * depth, depth, 1)
    partial = jnp.dot(cond_owned, ada_weight, preferred_element_type=jnp.float32)
    mod_rows = lax.psum_scatter(partial, "dp", scatter_dimension=0, tiled=True)
    mod_rows = mod_rows + ada_bias.astype(jnp.float32)
    bias_row = jnp.concatenate(own_biases).astype(jnp.float32)
    payload = jnp.concatenate(
        [mod_rows, jnp.broadcast_to(bias_row, (columns, bias_row.shape[0]))], axis=1
    )
    arrived = lax.all_to_all(payload, "fsdp", split_axis=0, concat_axis=0, tiled=True)
    modulation = arrived[:, :mod_width].reshape(1, -1)
    biases = tuple(
        arrived[:, cut : cut + width].reshape(-1) for cut, width in zip(cuts, widths)
    )

    shard = pack_shard(qkv_weight, proj_weight, fc1_weight, fc2_weight)
    blocks = gather_shards(shard, rows, columns)
    weights = unpack_full(blocks, qkv_weight.shape[1], fc2_weight.shape[1])
    block_out, latent_grad, mod_grad, weight_grads, bias_grads = layer(
        latents[0], cond_act, live, cotangent[0], modulation, weights, biases
    )
    grads = pack_full(weight_grads, columns, rows)
    owned = scatter_shards(grads)
    qkv_grad, proj_grad, fc1_grad, fc2_grad = unpack_shard(
        owned, qkv_weight.shape[1], fc2_weight.shape[1]
    )

    leaving = jnp.concatenate(
        [mod_grad.reshape(columns, -1)] + [grad.reshape(columns, -1) for grad in bias_grads], axis=1
    )
    group_rows = lax.all_to_all(leaving, "fsdp", split_axis=0, concat_axis=0, tiled=True)
    all_rows = lax.all_gather(group_rows, "dp", axis=0, tiled=True)
    mod_owned = all_rows[:, :mod_width]
    ada_grad = contract_exact(cond_owned.astype(jnp.float32), mod_owned)
    sums = jnp.sum(all_rows, axis=0)
    ada_bias_grad = sums[:mod_width]
    bias_sums = [sums[cut : cut + width] for cut, width in zip(cuts, widths)]
    back = lax.dot_general(
        mod_owned, ada_weight.astype(jnp.float32), (((1,), (1,)), ((), ())), precision=highest
    )
    back = lax.psum_scatter(
        back.reshape(rows, columns, depth), "fsdp", scatter_dimension=1, tiled=True
    )
    back = lax.all_to_all(
        back.reshape(rows, depth), "dp", split_axis=0, concat_axis=0, tiled=True
    ).reshape(1, -1)
    cond_grad = jax.vjp(jax.nn.silu, cond_row)[1](back)[0]
    return (
        block_out[None],
        latent_grad[None],
        cond_grad,
        ada_grad,
        ada_bias_grad,
        qkv_grad,
        bias_sums[0],
        proj_grad,
        bias_sums[1],
        fc1_grad,
        bias_sums[2],
        fc2_grad,
        bias_sums[3],
    )


def solution(mesh):
    in_specs = (
        P(("dp", "fsdp"), None, None),
        P(("dp", "fsdp"), None),
        P(("dp", "fsdp"), None, None),
        P(("dp", "fsdp")),
        P("dp", "fsdp"),
        P("fsdp"),
        P("dp", "fsdp"),
        P("fsdp"),
        P("dp", "fsdp"),
        P("fsdp"),
        P("dp", "fsdp"),
        P("fsdp"),
        P("dp", "fsdp"),
        P("fsdp"),
    )
    out_specs = (
        P(("dp", "fsdp"), None, None),
        P(("dp", "fsdp"), None, None),
        P(("dp", "fsdp"), None),
        P("dp", "fsdp"),
        P("fsdp"),
        P("dp", "fsdp"),
        P("fsdp"),
        P("dp", "fsdp"),
        P("fsdp"),
        P("dp", "fsdp"),
        P("fsdp"),
        P("dp", "fsdp"),
        P("fsdp"),
    )
    return jax.shard_map(
        per_device, mesh=mesh, in_specs=in_specs, out_specs=out_specs, check_vma=False
    )
```

time: 930 us -> 469 us (0.50)
  waiting for transfers between devices: 573 us -> 2.22 us
  Pallas kernels: 0 us -> 135 us
  local copies, waits for them, and re-layouts: 39.9 us -> 150 us
  blocking collectives: 183 us -> 77.3 us
  starting transfers between devices: 82.3 us -> 15.2 us
  matrix products: 24.5 us -> 49.9 us
  other arithmetic: 0.04 us -> 17.1 us
    all_gather x12 -> x0, waiting for transfers between devices: 357 us -> none  [the longest x1 90.5 us: per_device(): lax.all_gather(pairs[3], 'fsdp', axis=0, tiled=True)]
    pallas_call x0 -> x2, Pallas kernels: none -> 135 us  [the longest x1 68 us: scatter_shards(): pl.pallas_call(functools.partial(scatter_kernel, rows, depth), out_shape=...]
    reduce_scatter x5 -> x0, waiting for transfers between devices: 111 us -> none  [the longest x1 31.9 us: per_device(): lax.psum_scatter(folded[0], 'dp', scatter_dimension=0, tiled=True)]
    reshape x0 -> x25, local copies, waits for them, and re-layouts: none -> 99 us  [the longest x2 22.3 us: unpack_full(): blocks[:, :, 2 * height:].reshape(columns, rows, height, tall, low_width)]
    all_to_all x3, waiting for transfers between devices: 101 us -> 2.19 us  [the longest x1 2.18 us: per_device(): lax.all_to_all(back.reshape(rows, depth), 'dp', split_axis=0, concat_axis...]
    all_to_all x3, starting transfers between devices: 81.7 us -> 15.2 us  [the longest x1 6.64 us: per_device(): lax.all_to_all(payload, 'fsdp', split_axis=0, concat_axis=0, tiled=True)]
    all_gather x5 -> x2, blocking collectives: 91.2 us -> 51.3 us  [the longest x1 43.6 us: per_device(): cond_all = lax.all_gather(cond_act, ('dp', 'fsdp'), axis=0, tiled=True)]
    dot_general x0 -> x15, matrix products: none -> 33.9 us  [the longest x4 11.4 us: against_weight(): lax.dot_general(grad_rows, weight, (((1,), (1,)), ((), ())), preferred_el...]
  transfers between devices with their start and end apart: 20 -> 4, of which waited for: 13 -> 1; matrix products, arithmetic and copies ran while one was open for 5% -> 33% of each run, Pallas kernels for 0% -> 29%
where the time goes in v1:
time: 469 us; the launch traced here: 463 us
  local copies, waits for them, and re-layouts  150 us (32%)
  Pallas kernels  135 us (29%)
  blocking collectives  77.3 us (16%)
  matrix products  49.9 us (11%)
  other arithmetic  17.1 us (4%)
  between operations  16.4 us (3%)
  starting transfers between devices  15.2 us (3%)
    pallas_call x1, Pallas kernels, scatter_shards(): pl.pallas_call(functools.partial(scatter_kernel, rows, depth), out_shape=...  68 us
    pallas_call x1, Pallas kernels, gather_shards(): pl.pallas_call(functools.partial(gather_kernel, rows, depth), out_shape=j...  66.6 us
    all_gather x1, blocking collectives, per_device(): cond_all = lax.all_gather(cond_act, ('dp', 'fsdp'), axis=0, tiled=True)  43.6 us
    transpose x6, local copies, waits for them, and re-layouts, wide(): return part.transpose(1, 2, 0, 3).reshape(rows * height, -1)  29.3 us
    unnamed x1, blocking collectives  25.9 us
    reshape x2, local copies, waits for them, and re-layouts, unpack_full(): blocks[:, :, 2 * height:].reshape(columns, rows, height, tall, low_width)  22.3 us
    reshape x2, local copies, waits for them, and re-layouts, pack_full(): fc2.reshape(rows, tall, height, columns, -1).transpose(3, 0, 2, 1, 4)  21.8 us
    reshape x5, local copies, waits for them, and re-layouts, blocked(): return grad.reshape(rows, height, columns, -1).transpose(2, 0, 1, 3)  20.8 us
  transfers between devices with their start and end apart: 4, of which 1 were waited for; matrix products, arithmetic and copies ran while one was open for 33% of the time, Pallas kernels for 29%

profile of v1, /device:TPU:0, one launch (start us, length us, event | category | flops | bytes accessed | tf_op | source)
XLA Modules:
  0.0 462.8 jit_solution(1936598028152543085)
XLA Ops:
  7.2 0.8 convert_bitcast_fusion.1
  8.0 43.6 %all-gather.1 = bf16[32,1,768]{2,1,0:T(2,128)(2,1)S(1)} all-gather(bf16[1,1,768]{2,1,0:T(2,128)(2,1)S(1)} %get-tuple-element.34), channel_id=1, replica_groups=mesh['dp'=4,'fsdp'=8] {'dp','fsdp'}, dimensions={0}, use_global_device_ids=true | all-gather | bytes 50688 | tf_op jit(solution)/shard_map/all_gather | solution.py:480
  51.8 0.8 fusion.66
  52.6 1.1 reshape.233
  54.1 1.9 pad_maximum_fusion.2.shard
  56.0 66.6 %gather_shards.1 = bf16[8,4,576,384]{3,2,1,0:T(8,128)(2,1)} custom-call(bf16[576,384]{1,0:T(8,128)(2,1)} %pad_maximum_fusion.2.shard), custom_call_target="tpu_custom_call" | custom-call | tf_op jit(solution)/shard_map/gather_shards/pallas_call | solution.py:131
  122.5 5.1 %slice_bitcast_fusion.1 = bf16[4,192,8,288]{3,1,0,2:T(8,128)(2,1)} fusion(bf16[8,4,576,384]{3,2,1,0:T(8,128)(2,1)} %gather_shards.1), kind=kLoop, calls=%fused_computation.10 | loop fusion | bytes 7077888 | tf_op jit(solution)/shard_map/transpose | solution.py:427
  127.7 1.9 slice_bitcast_fusion.2
  129.7 8.8 %slice_bitcast_fusion = (bf16[4,192,8,384]{3,1,0,2:T(8,128)(2,1)}, bf16[8,4,192,384]{3,2,1,0:T(8,128)(2,1)}) fusion(bf16[8,4,576,384]{3,2,1,0:T(8,128)(2,1)} %gather_shards.1), kind=kLoop, calls=%fused_computation.9 | loop fusion | bytes 18874368 | tf_op jit(solution)/shard_map/transpose | solution.py:427
  140.3 0.7 dynamic-slice_add_fusion
  141.1 0.7 all_to_all.20
  141.7 6.6 %all-to-all-start = ((f32[8,1,1344]{2,1,0:T(1,128)}), f32[8,1,1344]{2,1,0:T(1,128)S(1)}, u32[]{:S(2)}, u32[]{:S(2)}) async-start(f32[8,1,1344]{2,1,0:T(1,128)} %all_to_all.20), calls=%async_computation | async-start | bytes 90112 | tf_op jit(solution)/shard_map/all_to_all | solution.py:489
  149.1 7.3 %copy.82 = bf16[4,192,8,288]{3,2,1,0:T(8,128)(2,1)} copy(bf16[4,192,8,288]{3,1,0,2:T(8,128)(2,1)} %slice_bitcast_fusion.1) | data formatting | bytes 7077888 | tf_op jit(solution)/shard_map/transpose | solution.py:427
  156.3 8.0 %reshape.235 = bf16[768,2304]{1,0:T(8,128)(2,1)} reshape(bf16[4,192,8,288]{3,2,1,0:T(8,128)(2,1)} %copy.82) | data formatting | bytes 7077888 | tf_op jit(solution)/shard_map/reshape | solution.py:427
  164.3 1.0 copy.87
  165.3 1.3 reshape.239
  166.7 5.2 %copy.88 = bf16[4,192,8,384]{3,2,1,0:T(8,128)(2,1)S(1)} copy(bf16[4,192,8,384]{3,1,0,2:T(8,128)(2,1)} %get-tuple-element.36) | data formatting | bytes 9437184 | tf_op jit(solution)/shard_map/transpose | solution.py:427
  171.8 3.3 copy.108
  175.1 12.7 %reshape.241 = bf16[8,4,192,4,96]{4,3,2,1,0:T(4,128)(2,1)} reshape(bf16[8,4,192,384]{3,2,1,0:T(8,128)(2,1)} %get-tuple-element.37) | data formatting | bytes 9437184 | tf_op jit(solution)/shard_map/reshape | solution.py:430
  187.9 9.5 %copy.121 = bf16[8,4,192,4,96]{4,0,2,3,1:T(8,128)(2,1)} copy(bf16[8,4,192,4,96]{4,3,2,1,0:T(4,128)(2,1)} %reshape.241) | data formatting | bytes 9437184 | tf_op jit(solution)/shard_map/reshape | solution.py:430
  197.4 10.9 %reshape.242 = bf16[3072,768]{1,0:T(8,128)(2,1)} reshape(bf16[4,4,192,8,96]{4,3,2,1,0:T(8,128)(2,1)} %bitcast.169) | data formatting | bytes 9437184 | tf_op jit(solution)/shard_map/reshape | solution.py:435
  209.5 3.2 fusion.1
  213.3 2.9 fusion.81
  216.2 2.3 convolution_convert_fusion.6
  218.6 0.8 copy-done.11
  220.2 4.0 convolution_add_fusion.1
  224.2 6.4 %convert_reduce_fusion = (f32[3072]{0:T(1024)S(1)}, bf16[256,3072]{1,0:T(8,128)(2,1)S(1)}) fusion(f32[256,3072]{1,0:T(8,128)S(1)} %convolution_add_fusion.1, bf16[3072,768]{1,0:T(8,128)(2,1)} %reshape.242, bf16[1,256,768]{2,1,0:T(8,128)(2,1)S(1)} %copy-done.24, f32[768]{0:T(1024)S(1)} %get-tuple-element.23, f32[]{:T(128)} %bitcast), kind=kOutput, calls=%fused_computation.23 | convolution fusion | flops 1226044416 | bytes 9845764 | tf_op jit(solution)/shard_map/dot_general | solution.py:289
  230.6 2.5 multiply_reduce_fusion.2
  233.2 6.7 %convert_reduce_fusion.3 = (f32[768]{0:T(1024)S(1)}, f32[768]{0:T(1024)S(1)}, bf16[1,256,768]{2,1,0:T(8,128)(2,1)}, f32[768]{0:T(1024)S(1)}, bf16[256,768]{1,0:T(8,128)(2,1)S(1)}, /*index=5*/f32[256,768]{1,0:T(8,128)}) fusion(bf16[1,256,768]{2,1,0:T(8,128)(2,1)} %param.16, f32[]{:T(128)} %bitcast, f32[768]{0:T(1024)S(1)} %get-tuple-element.23, ...), kind=kOutput, calls=%fused_computation.76 | convolution fusion | flops 1219950336 | bytes 11428868 | tf_op jit(solution)/shard_map/dot_general | solution.py:332
  239.9 0.8 copy-done.13
  240.7 1.3 convolution_convert_fusion.5
  241.9 1.2 copy.90
  243.1 2.8 convolution_convert_fusion.4
  246.0 0.7 multiply_reduce_fusion
  248.7 1.0 copy-done.3
  249.7 1.4 fusion.28
  251.7 4.5 convolution_convert_fusion
  256.3 3.7 convolution_convert_fusion.1
  260.5 3.1 convolution_convert_fusion.2
  263.7 1.1 multiply_reduce_fusion.3
  265.4 0.7 all_to_all.23
  266.1 5.3 %all-to-all-start.1 = ((f32[8,1,1344]{2,1,0:T(1,128)}), f32[8,1,1344]{2,1,0:T(1,128)S(1)}, u32[]{:S(2)}, u32[]{:S(2)}) async-start(f32[8,1,1344]{2,1,0:T(1,128)} %all_to_all.23), calls=%async_computation.1 | async-start | bytes 90112 | tf_op jit(solution)/shard_map/all_to_all | solution.py:510
  271.4 11.6 %reshape.256 = bf16[4,4,192,8,96]{4,3,2,1,0:T(8,128)(2,1)} reshape(bf16[3072,768]{1,0:T(8,128)(2,1)} %convolution_convert_fusion) | data formatting | bytes 9437184 | tf_op jit(solution)/shard_map/reshape | solution.py:447
  282.9 10.3 %copy.120 = bf16[4,4,192,8,96]{4,1,2,0,3:T(4,128)(2,1)} copy(bf16[4,4,192,8,96]{4,3,2,1,0:T(8,128)(2,1)} %reshape.256) | data formatting | bytes 9437184 | tf_op jit(solution)/shard_map/reshape | solution.py:447
  293.2 10.8 %reshape.257 = bf16[8,4,192,384]{3,2,1,0:T(8,128)(2,1)} reshape(bf16[8,4,192,4,96]{4,3,2,1,0:T(4,128)(2,1)} %bitcast.170) | data formatting | bytes 9437184 | tf_op jit(solution)/shard_map/reshape | solution.py:448
  304.0 3.5 copy.109
  307.5 3.0 copy.122
  310.5 2.6 reshape.254
  313.1 1.8 copy.124
  314.9 10.1 %reshape.253 = bf16[4,192,8,288]{3,2,1,0:T(8,128)(2,1)} reshape(bf16[768,2304]{1,0:T(8,128)(2,1)} %convolution_convert_fusion.2) | data formatting | bytes 7077888 | tf_op jit(solution)/shard_map/reshape | solution.py:444
  325.0 3.4 copy.123
  328.6 10.0 %pad_maximum_fusion.grads = bf16[8,4,576,384]{3,2,1,0:T(8,128)(2,1)} fusion(bf16[8,4,192,384]{3,2,1,0:T(8,128)(2,1)} %reshape.257, bf16[8,4,192,384]{3,2,1,0:T(8,128)(2,1)S(1)} %bitcast.173, bf16[8,4,192,96]{3,2,1,0:T(8,128)(2,1)S(1)} %bitcast.177, bf16[8,4,192,288]{3,2,1,0:T(8,128)(2,1)S(1)} %bitcast.174), kind=kLoop, calls=%fused_computation.1 | loop fusion | flops 56623104 | bytes 28311552 | tf_op jit(solution)/shard_map/concatenate | solution.py:450
  338.6 68.0 %scatter_shards.1 = f32[576,384]{1,0:T(8,128)S(1)} custom-call(bf16[8,4,576,384]{3,2,1,0:T(8,128)(2,1)} %pad_maximum_fusion.grads), custom_call_target="tpu_custom_call" | custom-call | tf_op jit(solution)/shard_map/scatter_shards/pallas_call | solution.py:244
  406.7 0.8 fusion.76
  407.4 0.7 slice.123
  408.2 0.7 slice.125
  409.4 1.0 reshape.259
  410.4 7.7 %all-gather = f32[32,1,1344]{2,1,0:T(1,128)S(1)} all-gather(f32[8,1,1344]{2,1,0:T(1,128)S(1)} %all-to-all-done.1), channel_id=2, replica_groups=mesh['dp'=4,'fsdp'=8] {'dp'}, dimensions={0}, use_global_device_ids=true | all-gather | bytes 215040 | tf_op jit(solution)/shard_map/all_gather | solution.py:511
  418.5 1.2 fusion.63
  419.9 25.9 %all-reduce.1 = f32[4,8,192]{2,0,1:T(4,128)S(1)} all-reduce(f32[4,8,192]{2,0,1:T(4,128)S(1)} %copy.94), channel_id=4, replica_groups=mesh['dp'=4,'fsdp'=8] {'fsdp'}, use_global_device_ids=true, to_apply=%region_22.23.clone | all-reduce | flops 6144 | bytes 49152
  445.8 0.6 constant_dynamic-slice_fusion
  447.1 3.2 all-to-all-start.2
  452.1 0.6 slice.146
  452.8 2.2 all-to-all-done.2
  (144 shorter events, 12.6 us)
Async XLA Ops:
  7.2 44.6 %copy-start = (bf16[192,576]{1,0:T(8,128)(2,1)S(1)}, bf16[192,576]{1,0:T(8,128)(2,1)}, u32[]{:S(2)}) copy-start(bf16[192,576]{1,0:T(8,128)(2,1)} %param.18) | copy-start | bytes 663556
  7.2 133.1 %all-reduce.4.cloned.1.call-start = ((), (), s32[]{:S(2)}) async-start(), calls=%async_computation.3 | async-start | bytes 163840
  129.6 8.8 %copy-start.19 = (bf16[576]{0:T(1024)(128)(2,1)S(1)}, bf16[576]{0:T(1024)(128)(2,1)}, u32[]{:S(2)}) copy-start(bf16[576]{0:T(1024)(128)(2,1)} %param.19) | copy-start | bytes 3460
  129.6 8.8 %copy-start.1 = (bf16[1,256,768]{2,1,0:T(8,128)(2,1)S(1)}, bf16[1,256,768]{2,1,0:T(8,128)(2,1)}, u32[]{:S(2)}) copy-start(bf16[1,256,768]{2,1,0:T(8,128)(2,1)} %param.14) | copy-start | bytes 1179652
  129.6 9.0 %copy-start.27 = (u32[32]{0:T(128)S(1)}, u32[32]{0:T(128)}, u32[]{:S(2)}) copy-start(u32[32]{0:T(128)} %constant.55) | copy-start | bytes 388
  129.7 10.2 %copy-start.20 = (bf16[384]{0:T(512)(128)(2,1)S(1)}, bf16[384]{0:T(512)(128)(2,1)}, u32[]{:S(2)}) copy-start(bf16[384]{0:T(512)(128)(2,1)} %param.25) | copy-start | bytes 2308
  129.7 10.2 %copy-start.21 = (bf16[96]{0:T(256)(128)(2,1)S(1)}, bf16[96]{0:T(256)(128)(2,1)}, u32[]{:S(2)}) copy-start(bf16[96]{0:T(256)(128)(2,1)} %param.27) | copy-start | bytes 580
  129.7 10.2 %copy-start.22 = (bf16[96]{0:T(256)(128)(2,1)S(1)}, bf16[96]{0:T(256)(128)(2,1)}, u32[]{:S(2)}) copy-start(bf16[96]{0:T(256)(128)(2,1)} %param.23) | copy-start | bytes 580
  129.7 10.2 %copy-start.23 = (bf16[192]{0:T(256)(128)(2,1)S(1)}, bf16[192]{0:T(256)(128)(2,1)}, u32[]{:S(2)}) copy-start(bf16[192]{0:T(256)(128)(2,1)} %param.21) | copy-start | bytes 1156
  141.7 67.1 %all-to-all-start = ((f32[8,1,1344]{2,1,0:T(1,128)}), f32[8,1,1344]{2,1,0:T(1,128)S(1)}, u32[]{:S(2)}, u32[]{:S(2)}) async-start(f32[8,1,1344]{2,1,0:T(1,128)} %all_to_all.20), calls=%async_computation | async-start | bytes 90112 | tf_op jit(solution)/shard_map/all_to_all | solution.py:489
  197.4 10.9 %copy-start.26 = (u32[32]{0:T(128)S(1)}, u32[32]{0:T(128)}, u32[]{:S(2)}) copy-start(u32[32]{0:T(128)} %constant.59) | copy-start | bytes 388
  197.4 12.1 %copy-start.2 = (bf16[1,256,768]{2,1,0:T(8,128)(2,1)S(1)}, bf16[1,256,768]{2,1,0:T(8,128)(2,1)}, u32[]{:S(2)}) copy-start(bf16[1,256,768]{2,1,0:T(8,128)(2,1)} %param.14) | copy-start | bytes 1179652
  212.9 5.6 %copy-start.16 = (bf16[256,768]{0,1:T(8,128)(2,1)}, bf16[256,768]{0,1:T(8,128)(2,1)S(1)}, u32[]{:S(2)}) copy-start(bf16[256,768]{0,1:T(8,128)(2,1)S(1)} %copy.83) | copy-start | bytes 1179652
  213.1 5.4 %copy-start.5 = (bf16[256,768]{0,1:T(8,128)(2,1)}, bf16[256,768]{0,1:T(8,128)(2,1)S(1)}, u32[]{:S(2)}) copy-start(bf16[256,768]{0,1:T(8,128)(2,1)S(1)} %copy.84) | copy-start | bytes 1179652
  213.3 5.3 %copy-start.7 = (bf16[256,768]{0,1:T(8,128)(2,1)}, bf16[256,768]{0,1:T(8,128)(2,1)S(1)}, u32[]{:S(2)}) copy-start(bf16[256,768]{0,1:T(8,128)(2,1)S(1)} %copy.85) | copy-start | bytes 1179652
  218.6 0.8 copy-start.11
  220.2 4.0 copy-start.24
  220.2 10.4 %slice-start.2 = ((s8[4718592]{0:T(1024)(128)(4,1)}), s8[4194304]{0:T(1024)(128)(4,1)S(1)}, s32[]{:S(2)}) async-start(s8[4718592]{0:T(1024)(128)(4,1)} %bitcast.179), calls=%async_computation.6 | async-start | bytes 8388608
  224.2 6.4 %copy-start.28 = (f32[256,3072]{1,0:T(8,128)}, f32[256,3072]{1,0:T(8,128)S(1)}, u32[]{:S(2)}) copy-start(f32[256,3072]{1,0:T(8,128)S(1)} %convolution_add_fusion.1) | copy-start | bytes 9437188
  224.2 6.4 %slice-start.3 = ((s8[4718592]{0:T(1024)(128)(4,1)}), s8[524288]{0:T(1024)(128)(4,1)S(1)}, s32[]{:S(2)}) async-start(s8[4718592]{0:T(1024)(128)(4,1)} %bitcast.179), calls=%async_computation.7 | async-start | bytes 1048576
  230.6 2.5 copy-start.9
  239.9 0.8 copy-start.13
  243.1 2.8 copy-start.4
  243.1 2.9 copy-start.17
  246.7 1.0 copy-start.6
  246.7 1.6 copy-start.8
  247.7 2.0 copy-start.3
  249.7 1.8 copy-start.25
  249.7 2.0 copy-start.29
  251.7 4.5 copy-start.10
  256.3 3.8 copy-start.12
  256.3 3.8 copy-start.14
  260.5 3.2 copy-start.15
  266.1 144.3 %all-to-all-start.1 = ((f32[8,1,1344]{2,1,0:T(1,128)}), f32[8,1,1344]{2,1,0:T(1,128)S(1)}, u32[]{:S(2)}, u32[]{:S(2)}) async-start(f32[8,1,1344]{2,1,0:T(1,128)} %all_to_all.23), calls=%async_computation.1 | async-start | bytes 90112 | tf_op jit(solution)/shard_map/all_to_all | solution.py:510
  314.9 13.5 %slice-start = ((s8[4718592]{0:T(1024)(128)(4,1)}), s8[524288]{0:T(1024)(128)(4,1)S(1)}, s32[]{:S(2)}) async-start(s8[4718592]{0:T(1024)(128)(4,1)} %bitcast.171), calls=%async_computation.4 | async-start | bytes 1048576
  325.0 3.6 slice-start.1
  406.7 48.4 %copy-start.18 = (bf16[1,768]{1,0:T(2,128)(2,1)S(1)}, bf16[1,768]{1,0:T(2,128)(2,1)}, u32[]{:S(2)}) copy-start(bf16[1,768]{1,0:T(2,128)(2,1)} %param.15) | copy-start | bytes 4612
  447.1 7.9 %all-to-all-start.2 = ((f32[4,1,192]{2,1,0:T(1,128)}), f32[4,1,192]{2,1,0:T(1,128)S(1)}, u32[]{:S(2)}, u32[]{:S(2)}) async-start(f32[4,1,192]{2,1,0:T(1,128)} %copy.95), calls=%async_computation.2 | async-start | bytes 8192 | tf_op jit(solution)/shard_map/all_to_all | solution.py:523
Sparse Core Ops, SparseCore 0:
  52.7 37.9 all-reduce.3

commit v2 on v1

v2 whole, which is shorter than its diff:
```python
import functools
import jax
import jax.numpy as jnp
from jax import lax
from jax.sharding import PartitionSpec as P
from jax.experimental import pallas as pl
from jax.experimental.pallas import tpu as pltpu

MESH_IDS = pl.DeviceIdType.MESH
D = 768
HEADS = 12
HEAD = 64
FF = 3072

highest = lax.Precision.HIGHEST
bfloat = jnp.bfloat16


def place(dp_index, z_index, core):
    return (dp_index, z_index * 2 + core)


def z_order(size):
    steps = [0]
    for distance in range(1, size // 2 + 1):
        steps.append(distance)
        if size - distance != distance:
            steps.append(size - distance)
    return steps


def enter_barrier(partners):
    barrier = pltpu.get_barrier_semaphore()
    for partner in partners:
        pl.semaphore_signal(barrier, inc=1, device_id=partner, device_id_type=MESH_IDS)
    pl.semaphore_wait(barrier, len(partners))


def positions(rows, depth):
    dp = lax.axis_index("dp")
    column = lax.axis_index("fsdp")
    z, core = column // 2, column % 2
    others = [(dp ^ 1), (dp ^ 2)] if rows == 4 else [(dp + step) % rows for step in range(1, rows)]
    partners = [place(dp, z, 1 - core)]
    partners += [place(other, z, core) for other in others]
    partners += [place(dp, (z + step) % depth, core) for step in z_order(depth)[1:]]
    return dp, z, core, others, partners


def block_of(array, line, row, shape, turned):
    if len(array.shape) == 4:
        return array.at[line, row]
    high, wide = (line, row) if turned else (row, line)
    height, width = shape
    return array.at[
        pl.ds(pl.multiple_of(high * height, height), height),
        pl.ds(pl.multiple_of(wide * width, width), width),
    ]


def whole_shape(shape, turned, rows, columns):
    height, width = shape
    if width % 128 == 0 and height % 32 == 0:
        return (columns * height, rows * width) if turned else (rows * height, columns * width)
    return (columns, rows, height, width)


def gather_kernel(rows, depth, *refs):
    shards, outs = refs[:3], refs[3:6]
    own_sems, send_sems, recv_sems = refs[6:]
    dp, z, core, others, partners = positions(rows, depth)
    sibling = place(dp, z, 1 - core)
    enter_barrier(partners)
    sends = []

    def slot_of(part, line, row):
        return block_of(outs[part], line, row, shards[part].shape, part == 2)

    def half_of(ref, part, which):
        half = shards[part].shape[0] // 2
        return ref.at[pl.ds(which * half, half)]

    def send(line, row, target, which=None, own=False):
        for part in range(3):
            destination = slot_of(part, line, row)
            source = shards[part] if own else destination
            if which is not None:
                source, destination = half_of(source, part, which), half_of(destination, part, which)
            copy = pltpu.make_async_remote_copy(
                src_ref=source,
                dst_ref=destination,
                send_sem=send_sems.at[len(sends)],
                recv_sem=recv_sems.at[which or 0, part, line, row],
                device_id=target,
                device_id_type=MESH_IDS,
            )
            copy.start()
            sends.append(copy)

    def arrive(line, row, which=None):
        for part in range(3):
            destination = slot_of(part, line, row)
            if which is not None:
                destination = half_of(destination, part, which)
            pltpu.make_async_remote_copy(
                src_ref=destination,
                dst_ref=destination,
                send_sem=send_sems.at[0],
                recv_sem=recv_sems.at[which or 0, part, line, row],
                device_id=sibling,
                device_id_type=MESH_IDS,
            ).wait_recv()

    own = z * 2 + core
    steps = z_order(depth)
    lines = [((z - step) % depth) * 2 + core for step in steps]
    for other in others:
        send(own, dp, place(other, z, core), own=True)
    for step in steps[1:]:
        send(own, dp, place(dp, (z + step) % depth, core), own=True)
    send(own, dp, sibling, own=True)
    keeps = [
        pltpu.make_async_copy(shards[part], slot_of(part, own, dp), own_sems.at[part])
        for part in range(3)
    ]
    for keep in keeps:
        keep.start()
    for turn in range(depth + 2):
        if 0 < turn < depth:
            line = lines[turn]
            arrive(line, dp)
            for other in others:
                send(line, dp, place(other, z, core))
            send(line, dp, sibling)
        if 1 <= turn <= depth:
            line = lines[turn - 1]
            for position, other in enumerate(others):
                arrive(line, other)
                if rows == 4:
                    send(line, other, place(others[1 - position], z, core), which=position)
                send(line, other, sibling)
        if turn >= 2 and rows == 4:
            line = lines[turn - 2]
            arrive(line, dp ^ 3, 0)
            arrive(line, dp ^ 3, 1)
            send(line, dp ^ 3, sibling)
    for line in lines:
        for row in range(rows):
            arrive(line + 1 - 2 * core, (dp + row) % rows)
    for keep in keeps:
        keep.wait()
    for copy in sends:
        copy.wait_send()


def gather_shards(shards, rows, columns):
    depth = columns // 2
    count = (depth - 1) + depth * rows + depth * (rows - 1) + (2 * depth if rows == 4 else 0)
    shapes = [
        whole_shape(shard.shape, part == 2, rows, columns) for part, shard in enumerate(shards)
    ]
    return pl.pallas_call(
        functools.partial(gather_kernel, rows, depth),
        out_shape=[jax.ShapeDtypeStruct(shape, bfloat) for shape in shapes],
        in_specs=[pl.BlockSpec(memory_space=pl.ANY)] * 3,
        out_specs=[pl.BlockSpec(memory_space=pl.ANY)] * 3,
        scratch_shapes=[
            pltpu.SemaphoreType.DMA((3,)),
            pltpu.SemaphoreType.DMA((3 * count,)),
            pltpu.SemaphoreType.DMA((2, 3, columns, rows)),
        ],
        compiler_params=pltpu.CompilerParams(collective_id=0, has_side_effects=True),
        name="gather_shards",
    )(*shards)


def scatter_kernel(rows, depth, *refs):
    grads, outs = refs[:3], refs[3:6]
    helds, pairs_in, planes_in, crosses_in, alongs_in = (
        refs[6 + 3 * kind : 9 + 3 * kind] for kind in range(5)
    )
    (
        load_sems, pair_send, pair_recv, plane_send, plane_recv,
        cross_send, cross_recv, along_send, along_recv,
    ) = refs[21:]
    dp, z, core, others, partners = positions(rows, depth)
    sibling = place(dp, z, 1 - core)
    targets = [dp ^ 3, dp ^ 1, dp ^ 2, dp] if rows == 4 else others + [dp]
    steps = z_order(depth)[::-1]
    enter_barrier(partners)
    waits = []

    def remote(source, destination, send_sem, recv_sem, target):
        copy = pltpu.make_async_remote_copy(
            src_ref=source, dst_ref=destination, send_sem=send_sem, recv_sem=recv_sem,
            device_id=target, device_id_type=MESH_IDS,
        )
        copy.start()
        waits.append(copy)
        return copy

    def add(first, others_in, length, target):
        chunk = 48 if length % 48 == 0 else 16

        @pl.loop(0, length // chunk)
        def _(index):
            piece = pl.ds(pl.multiple_of(index * chunk, chunk), chunk)
            total = first[piece, :].astype(jnp.float32)
            for other in others_in:
                total = total + other[piece, :].astype(jnp.float32)
            target[piece, :] = total.astype(target.dtype)

    lines = [(z + step) % depth for step in steps]
    pairs, loads, planes, crosses, alongs = {}, {}, {}, {}, {}
    for turn, line in enumerate(lines):
        for slot, target in enumerate(targets):
            for part in range(3):
                key = (part, turn, slot)
                shape = outs[part].shape
                pairs[key] = remote(
                    block_of(grads[part], line * 2 + 1 - core, target, shape, part == 2),
                    pairs_in[part].at[turn, slot], pair_send.at[key], pair_recv.at[key], sibling)
                loads[key] = pltpu.make_async_copy(
                    block_of(grads[part], line * 2 + core, target, shape, part == 2),
                    helds[part].at[turn, slot], load_sems.at[key])
                loads[key].start()
    last = len(targets) - 1
    for turn in range(depth + 2):
        if turn < depth:
            for slot in range(len(targets)):
                for part in range(3):
                    key = (part, turn, slot)
                    height = outs[part].shape[0]
                    half = height // 2
                    loads[key].wait()
                    pairs[key].wait_recv()
                    here = helds[part].at[turn, slot]
                    add(here, [pairs_in[part].at[turn, slot]], height, here)
                    if rows == 4 and slot == 0:
                        for position in range(2):
                            key = (part, turn, position)
                            crosses[key] = remote(
                                helds[part].at[turn, 0, pl.ds((1 - position) * half, half)],
                                crosses_in[part].at[turn, position],
                                cross_send.at[key], cross_recv.at[key],
                                place(others[position], z, core))
                    if rows != 4 and slot < last:
                        planes[key] = remote(
                            here, planes_in[part].at[turn, slot], plane_send.at[key],
                            plane_recv.at[key], place(targets[slot], z, core))
        if rows == 4 and 1 <= turn <= depth:
            now = turn - 1
            for position in range(2):
                for part in range(3):
                    half = outs[part].shape[0] // 2
                    crosses[part, now, 1 - position].wait_recv()
                    piece = helds[part].at[now, 1 + position, pl.ds(position * half, half)]
                    add(piece, [crosses_in[part].at[now, 1 - position]], half, piece)
                    key = (part, now, position)
                    planes[key] = remote(
                        helds[part].at[now, 1 + position], planes_in[part].at[now, position],
                        plane_send.at[key], plane_recv.at[key],
                        place(others[position], z, core))
        if turn >= 2:
            now = turn - 2
            for part in range(3):
                for slot in range(len(others)):
                    planes[part, now, slot].wait_recv()
                here = helds[part].at[now, last]
                arrived = [planes_in[part].at[now, slot] for slot in range(len(others))]
                add(here, arrived, outs[part].shape[0], here)
                if now < depth - 1:
                    key = (part, now)
                    alongs[key] = remote(
                        here, alongs_in[part].at[now], along_send.at[key], along_recv.at[key],
                        place(dp, lines[now], core))
    for part in range(3):
        for now in range(depth - 1):
            alongs[part, now].wait_recv()
        arrived = [alongs_in[part].at[now] for now in range(depth - 1)]
        add(helds[part].at[depth - 1, last], arrived, outs[part].shape[0], outs[part])
    for copy in waits:
        copy.wait_send()


def scatter_shards(grads, shapes, rows, columns):
    depth = columns // 2
    peers = 2 if rows == 4 else rows - 1
    dma = pltpu.SemaphoreType.DMA
    buffers = []
    for lead in ((depth, rows), (depth, rows), (depth, peers), (depth, 2), (depth - 1,)):
        for height, width in shapes:
            if lead == (depth, 2) and len(buffers) >= 9:
                height = height // 2 if rows == 4 else 16
            buffers.append(pltpu.VMEM(lead + (height, width), bfloat))
    return pl.pallas_call(
        functools.partial(scatter_kernel, rows, depth),
        out_shape=[jax.ShapeDtypeStruct(shape, jnp.float32) for shape in shapes],
        in_specs=[pl.BlockSpec(memory_space=pl.ANY)] * 3,
        out_specs=[pl.BlockSpec(memory_space=pltpu.VMEM)] * 3,
        scratch_shapes=buffers + [
            dma((3, depth, rows)), dma((3, depth, rows)), dma((3, depth, rows)),
            dma((3, depth, peers)), dma((3, depth, peers)),
            dma((3, depth, 2)), dma((3, depth, 2)),
            dma((3, depth - 1)), dma((3, depth - 1)),
        ],
        compiler_params=pltpu.CompilerParams(
            collective_id=1, has_side_effects=True, vmem_limit_bytes=50 * 2**20),
        name="scatter_shards",
    )(*grads)


def normalize_rows(values):
    center = jnp.mean(values, axis=-1, keepdims=True)
    spread = jnp.mean(jnp.square(values - center), axis=-1, keepdims=True)
    inverse = lax.rsqrt(spread + 1e-06)
    return ((values - center) * inverse, inverse)


def norm_backward(grad_normed, normed, inverse):
    centered = grad_normed - jnp.mean(grad_normed, axis=-1, keepdims=True)
    return inverse * (centered - normed * jnp.mean(grad_normed * normed, axis=-1, keepdims=True))


def contract_rows(left_rows, right_rows):
    return lax.dot_general(
        left_rows, right_rows, (((0,), (0,)), ((), ())), preferred_element_type=jnp.float32
    )


def contract_exact(left_rows, right_rows):
    return lax.dot_general(left_rows, right_rows, (((0,), (0,)), ((), ())), precision=highest)


def against_weight(grad_rows, weight):
    return lax.dot_general(
        grad_rows, weight, (((1,), (1,)), ((), ())), preferred_element_type=jnp.float32
    )


def pick(mixed, columns, kind):
    width = mixed.shape[1] // columns
    edge = 3 * width // 4
    low, high = (0, edge) if kind == 0 else (edge, width)
    return jnp.concatenate(
        [mixed[:, block * width + low : block * width + high] for block in range(columns)], axis=1
    )


def spread(rows_in, columns, kind):
    width = rows_in.shape[1] // columns
    rest = width // 3 if kind == 0 else 3 * width
    zeros = jnp.zeros((rows_in.shape[0], rest), rows_in.dtype)
    pieces = []
    for block in range(columns):
        piece = rows_in[:, block * width : (block + 1) * width]
        pieces += [piece, zeros] if kind == 0 else [zeros, piece]
    return jnp.concatenate(pieces, axis=1)


def layer(latent_rows, cond_act, live, cot_rows, modulation, weights, biases, columns):
    mixed_weight, fc1_weight, fc2_turned = weights
    qv_bias, proj_bias, fc1_bias, fc2_bias = biases
    length = latent_rows.shape[0]
    rows_wide = latent_rows.astype(jnp.float32)
    shift_one, scale_one, gate_one, shift_two, scale_two, gate_two = jnp.split(
        modulation, 6, axis=-1
    )
    normed_one, inverse_one = normalize_rows(rows_wide)
    hidden_one = (normed_one * (1.0 + scale_one) + shift_one).astype(bfloat)
    qkv_bias = jnp.concatenate([qv_bias[:D], jnp.zeros((D,), jnp.float32), qv_bias[D:]])
    projected = (
        pick(jnp.dot(hidden_one, mixed_weight, preferred_element_type=jnp.float32), columns, 0)
        + qkv_bias
    ).astype(bfloat)
    queries = projected[:, :D].reshape(length, HEADS, HEAD)
    key_rows = projected[:, D : 2 * D].reshape(length, HEADS, HEAD)
    values = projected[:, 2 * D :].reshape(length, HEADS, HEAD)
    scale_factor = HEAD ** (-0.5)
    scores = (
        jnp.einsum("qhe,khe->hqk", queries, key_rows, preferred_element_type=jnp.float32)
        * scale_factor
    )
    row_max = jnp.max(scores, axis=-1, keepdims=True)
    shifted = jnp.exp(scores - row_max)
    row_total = jnp.sum(shifted, axis=-1, keepdims=True)
    exact_probability = shifted / row_total
    probability = exact_probability.astype(bfloat)
    attended = jnp.einsum("hqk,khe->qhe", probability, values, preferred_element_type=jnp.float32)
    attended = attended.reshape(length, D).astype(bfloat)
    branch = pick(jnp.dot(attended, mixed_weight, preferred_element_type=jnp.float32), columns, 1)
    branch = branch + proj_bias
    middle = rows_wide + gate_one * branch
    normed_two, inverse_two = normalize_rows(middle)
    hidden_two = (normed_two * (1.0 + scale_two) + shift_two).astype(bfloat)
    pre_gelu = jnp.dot(hidden_two, fc1_weight, preferred_element_type=jnp.float32) + fc1_bias
    activated, gelu_pull = jax.vjp(
        lambda argument: jax.nn.gelu(argument, approximate=True), pre_gelu
    )
    activated = activated.astype(bfloat)
    mlp_out = against_weight(activated, fc2_turned) + fc2_bias
    block_out = (live * (middle + gate_two * mlp_out)).astype(bfloat)

    grad_out = live * cot_rows.astype(jnp.float32)
    gate_two_grad = jnp.sum(grad_out * mlp_out, axis=0, keepdims=True)
    grad_mlp = (gate_two * grad_out).astype(bfloat)
    fc2_bias_grad = jnp.sum(grad_mlp.astype(jnp.float32), axis=0)
    grad_act = jnp.dot(grad_mlp, fc2_turned, preferred_element_type=jnp.float32)
    grad_pre = gelu_pull(grad_act)[0].astype(bfloat)
    fc1_bias_grad = jnp.sum(grad_pre.astype(jnp.float32), axis=0)
    grad_hidden_two = against_weight(grad_pre, fc1_weight)
    shift_two_grad = jnp.sum(grad_hidden_two, axis=0, keepdims=True)
    scale_two_grad = jnp.sum(grad_hidden_two * normed_two, axis=0, keepdims=True)
    grad_middle = grad_out + norm_backward(
        grad_hidden_two * (1.0 + scale_two), normed_two, inverse_two
    )
    gate_one_grad = jnp.sum(grad_middle * branch, axis=0, keepdims=True)
    grad_branch = (gate_one * grad_middle).astype(bfloat)
    proj_bias_grad = jnp.sum(grad_branch.astype(jnp.float32), axis=0)
    spread_branch = spread(grad_branch, columns, 1)
    grad_attended = (
        against_weight(spread_branch, mixed_weight).astype(bfloat).reshape(length, HEADS, HEAD)
    )
    grad_prob = jnp.einsum(
        "qhe,khe->hqk", grad_attended, values, preferred_element_type=jnp.float32
    )
    inner_sum = jnp.sum(exact_probability * grad_prob, axis=-1, keepdims=True)
    grad_scores = (exact_probability * (grad_prob - inner_sum)).astype(bfloat)
    grad_queries = (
        jnp.einsum("hqk,khe->qhe", grad_scores, key_rows, preferred_element_type=jnp.float32)
        * scale_factor
    )
    grad_keys = (
        jnp.einsum("hqk,qhe->khe", grad_scores, queries, preferred_element_type=jnp.float32)
        * scale_factor
    )
    grad_values = jnp.einsum(
        "hqk,qhe->khe", probability, grad_attended, preferred_element_type=jnp.float32
    )
    grad_projected = jnp.concatenate(
        [
            grad_queries.reshape(length, D),
            grad_keys.reshape(length, D),
            grad_values.reshape(length, D),
        ],
        axis=1,
    ).astype(bfloat)
    summed = jnp.sum(grad_projected.astype(jnp.float32), axis=0)
    qv_bias_grad = jnp.concatenate([summed[:D], summed[2 * D :]])
    spread_projected = spread(grad_projected, columns, 0)
    grad_hidden_one = against_weight(spread_projected, mixed_weight)
    shift_one_grad = jnp.sum(grad_hidden_one, axis=0, keepdims=True)
    scale_one_grad = jnp.sum(grad_hidden_one * normed_one, axis=0, keepdims=True)
    latent_grad = (
        grad_middle + norm_backward(grad_hidden_one * (1.0 + scale_one), normed_one, inverse_one)
    ).astype(bfloat)
    mod_grad = jnp.concatenate(
        [
            shift_one_grad,
            scale_one_grad,
            gate_one_grad,
            shift_two_grad,
            scale_two_grad,
            gate_two_grad,
        ],
        axis=-1,
    )
    weight_grads = (
        contract_rows(
            jnp.concatenate([hidden_one, attended]),
            jnp.concatenate([spread_projected, spread_branch]),
        ).astype(bfloat),
        contract_rows(hidden_two, grad_pre).astype(bfloat),
        contract_rows(grad_mlp, activated).astype(bfloat),
    )
    bias_grads = (qv_bias_grad, proj_bias_grad, fc1_bias_grad, fc2_bias_grad)
    return block_out, latent_grad, mod_grad, weight_grads, bias_grads


def flatten_blocks(blocks, turned):
    if blocks.ndim == 2:
        return blocks
    columns, rows, height, width = blocks.shape
    if turned:
        return blocks.transpose(0, 2, 1, 3).reshape(columns * height, rows * width)
    return blocks.transpose(1, 2, 0, 3).reshape(rows * height, columns * width)


def cut_blocks(whole, shape, turned, rows, columns):
    if len(whole_shape(shape, turned, rows, columns)) == 2:
        return whole
    height, width = shape
    if turned:
        return whole.reshape(columns, height, rows, width).transpose(0, 2, 1, 3)
    return whole.reshape(rows, height, columns, width).transpose(2, 0, 1, 3)


def per_device(
    latents,
    conditioning,
    cotangent,
    latent_count,
    ada_weight,
    ada_bias,
    qkv_weight,
    qv_bias,
    proj_weight,
    proj_bias,
    fc1_weight,
    fc1_bias,
    fc2_weight,
    fc2_bias,
):
    rows, columns = lax.axis_size("dp"), lax.axis_size("fsdp")
    row_index = lax.axis_index("dp")
    live = latent_count[0].astype(jnp.float32)
    depth = ada_weight.shape[0]
    mod_width = ada_weight.shape[1]
    own_biases = (qv_bias, proj_bias, fc1_bias, fc2_bias)
    widths = [bias.shape[0] for bias in own_biases]
    cuts = [mod_width + sum(widths[:place]) for place in range(len(widths))]

    cond_row = conditioning.astype(jnp.float32)
    cond_act = jax.nn.silu(cond_row).astype(bfloat)
    cond_all = lax.all_gather(cond_act, ("dp", "fsdp"), axis=0, tiled=True)
    cond_owned = lax.dynamic_slice_in_dim(cond_all, row_index * depth, depth, 1)
    partial = jnp.dot(cond_owned, ada_weight, preferred_element_type=jnp.float32)
    mod_rows = lax.psum_scatter(partial, "dp", scatter_dimension=0, tiled=True)
    mod_rows = mod_rows + ada_bias.astype(jnp.float32)
    bias_row = jnp.concatenate(own_biases).astype(jnp.float32)
    payload = jnp.concatenate(
        [mod_rows, jnp.broadcast_to(bias_row, (columns, bias_row.shape[0]))], axis=1
    )
    arrived = lax.all_to_all(payload, "fsdp", split_axis=0, concat_axis=0, tiled=True)
    modulation = arrived[:, :mod_width].reshape(1, -1)
    biases = tuple(
        arrived[:, cut : cut + width].reshape(-1) for cut, width in zip(cuts, widths)
    )

    qkv_width = qkv_weight.shape[1]
    shards = (
        jnp.concatenate([qkv_weight, proj_weight], axis=1),
        fc1_weight,
        fc2_weight.T,
    )
    shapes = [shard.shape for shard in shards]
    blocks = gather_shards(shards, rows, columns)
    weights = [flatten_blocks(block, part == 2) for part, block in enumerate(blocks)]
    block_out, latent_grad, mod_grad, weight_grads, bias_grads = layer(
        latents[0], cond_act, live, cotangent[0], modulation, weights, biases, columns
    )
    grads = [
        cut_blocks(grad, shapes[part], part == 2, rows, columns)
        for part, grad in enumerate(weight_grads)
    ]
    mixed_grad, fc1_grad, fc2_turned_grad = scatter_shards(grads, shapes, rows, columns)
    qkv_grad, proj_grad = mixed_grad[:, :qkv_width], mixed_grad[:, qkv_width:]
    fc2_grad = fc2_turned_grad.T

    leaving = jnp.concatenate(
        [mod_grad.reshape(columns, -1)] + [grad.reshape(columns, -1) for grad in bias_grads], axis=1
    )
    group_rows = lax.all_to_all(leaving, "fsdp", split_axis=0, concat_axis=0, tiled=True)
    all_rows = lax.all_gather(group_rows, "dp", axis=0, tiled=True)
    mod_owned = all_rows[:, :mod_width]
    ada_grad = contract_exact(cond_owned.astype(jnp.float32), mod_owned)
    sums = jnp.sum(all_rows, axis=0)
    ada_bias_grad = sums[:mod_width]
    bias_sums = [sums[cut : cut + width] for cut, width in zip(cuts, widths)]
    back = lax.dot_general(
        mod_owned, ada_weight.astype(jnp.float32), (((1,), (1,)), ((), ())), precision=highest
    )
    back = lax.psum_scatter(
        back.reshape(rows, columns, depth), "fsdp", scatter_dimension=1, tiled=True
    )
    back = lax.all_to_all(
        back.reshape(rows, depth), "dp", split_axis=0, concat_axis=0, tiled=True
    ).reshape(1, -1)
    cond_grad = jax.vjp(jax.nn.silu, cond_row)[1](back)[0]
    return (
        block_out[None],
        latent_grad[None],
        cond_grad,
        ada_grad,
        ada_bias_grad,
        qkv_grad,
        bias_sums[0],
        proj_grad,
        bias_sums[1],
        fc1_grad,
        bias_sums[2],
        fc2_grad,
        bias_sums[3],
    )


def solution(mesh):
    in_specs = (
        P(("dp", "fsdp"), None, None),
        P(("dp", "fsdp"), None),
        P(("dp", "fsdp"), None, None),
        P(("dp", "fsdp")),
        P("dp", "fsdp"),
        P("fsdp"),
        P("dp", "fsdp"),
        P("fsdp"),
        P("dp", "fsdp"),
        P("fsdp"),
        P("dp", "fsdp"),
        P("fsdp"),
        P("dp", "fsdp"),
        P("fsdp"),
    )
    out_specs = (
        P(("dp", "fsdp"), None, None),
        P(("dp", "fsdp"), None, None),
        P(("dp", "fsdp"), None),
        P("dp", "fsdp"),
        P("fsdp"),
        P("dp", "fsdp"),
        P("fsdp"),
        P("dp", "fsdp"),
        P("fsdp"),
        P("dp", "fsdp"),
        P("fsdp"),
        P("dp", "fsdp"),
        P("fsdp"),
    )
    return jax.shard_map(
        per_device, mesh=mesh, in_specs=in_specs, out_specs=out_specs, check_vma=False
    )
```

time: 469 us -> 364 us (0.78); the launches traced: 463 us -> 363 us
  local copies, waits for them, and re-layouts: 150 us -> 38.2 us
  matrix products: 49.9 us -> 62.3 us
  waiting for transfers between devices: 2.22 us -> 7.37 us
    reshape x18 -> x0, local copies, waits for them, and re-layouts: 98.6 us -> none  [the longest x2 22.3 us: unpack_full(): blocks[:, :, 2 * height:].reshape(columns, rows, height, tall, low_width)]
    transpose x7 -> x0, local copies, waits for them, and re-layouts: 29.5 us -> none  [the longest x6 29.3 us: wide(): return part.transpose(1, 2, 0, 3).reshape(rows * height, -1)]
    concatenate x2 -> x1, other arithmetic: 11.9 us -> 1.69 us  [per_device(): jnp.concatenate([qkv_weight, proj_weight], axis=1)]
    unnamed x80 -> x151, local copies, waits for them, and re-layouts: 12.3 us -> 18.5 us
    dot_general x4, matrix products: 11.4 us -> 17.1 us  [against_weight(): lax.dot_general(grad_rows, weight, (((1,), (1,)), ((), ())), preferred_el...]
    all_to_all x1, waiting for transfers between devices: 0.01 us -> 5.15 us  [per_device(): lax.all_to_all(payload, 'fsdp', split_axis=0, concat_axis=0, tiled=True)]
    dot_general x4 -> x3, matrix products: 11.9 us -> 15.9 us  [contract_rows(): lax.dot_general(left_rows, right_rows, (((0,), (0,)), ((), ())), preferre...]
  transfers between devices with their start and end apart: 4 -> 4, of which waited for: 1 -> 2; matrix products, arithmetic and copies ran while one was open for 33% -> 5% of each run, Pallas kernels for 29% -> 37%
where the time goes in v2:
time: 364 us; the launch traced here: 363 us
  Pallas kernels  135 us (37%)
  blocking collectives  78.2 us (21%)
  matrix products  62.3 us (17%)
  local copies, waits for them, and re-layouts  38.2 us (10%)
  between operations  16.4 us (5%)
  starting transfers between devices  13 us (4%)
  other arithmetic  13 us (4%)
  waiting for transfers between devices  7.37 us (2%)
    pallas_call x1, Pallas kernels, gather_shards(): pl.pallas_call(functools.partial(gather_kernel, rows, depth), out_shape=[...  68.2 us
    pallas_call x1, Pallas kernels, scatter_shards(): pl.pallas_call(functools.partial(scatter_kernel, rows, depth), out_shape=...  66.5 us
    all_gather x1, blocking collectives, per_device(): cond_all = lax.all_gather(cond_act, ('dp', 'fsdp'), axis=0, tiled=True)  43.6 us
    unnamed x1, blocking collectives  25.9 us
    unnamed x151, local copies, waits for them, and re-layouts  18.5 us
    dot_general x4, matrix products, against_weight(): lax.dot_general(grad_rows, weight, (((1,), (1,)), ((), ())), preferred_el...  17.1 us
    dot_general x3, matrix products, contract_rows(): lax.dot_general(left_rows, right_rows, (((0,), (0,)), ((), ())), preferre...  15.9 us
    all_gather x1, blocking collectives, per_device(): all_rows = lax.all_gather(group_rows, 'dp', axis=0, tiled=True)  8.71 us
  transfers between devices with their start and end apart: 4, of which 2 were waited for; matrix products, arithmetic and copies ran while one was open for 5% of the time, Pallas kernels for 37%

profile of v2, /device:TPU:0, one launch (start us, length us, event | category | flops | bytes accessed | tf_op | source)
XLA Modules:
  0.0 363.2 jit_solution(4353695455945252596)
XLA Ops:
  7.3 1.4 convert_bitcast_fusion.1
  8.6 43.6 %all-gather.1 = bf16[32,1,768]{2,1,0:T(2,128)(2,1)S(1)} all-gather(bf16[1,1,768]{2,1,0:T(2,128)(2,1)S(1)} %get-tuple-element.46), channel_id=1, replica_groups=mesh['dp'=4,'fsdp'=8] {'dp','fsdp'}, dimensions={0}, use_global_device_ids=true | all-gather | bytes 50688 | tf_op jit(solution)/shard_map/all_gather | solution.py:525
  52.3 0.8 fusion.55
  53.8 0.7 convert_element_type.103
  54.5 1.1 convert_reduce_fusion.2
  55.7 1.2 fusion.33
  56.9 1.2 dynamic-slice.1
  58.2 1.3 dynamic-slice.3
  60.1 0.8 maximum_convert_fusion
  61.0 1.7 pad_maximum_fusion.2.refs_0_
  62.6 68.2 %gather_shards.1 = (bf16[768,3072]{1,0:T(8,128)(2,1)}, bf16[768,3072]{1,0:T(8,128)(2,1)}, bf16[768,3072]{1,0:T(8,128)(2,1)}) custom-call(bf16[192,384]{1,0:T(8,128)(2,1)} %pad_maximum_fusion.2.refs_0_, bf16[192,384]{1,0:T(8,128)(2,1)} %refs_1_.1, bf16[96,768]{1,0:T(8,128)(2,1)} %bitcast.159), custom_call_target="tpu_custom_call" | custom-call | tf_op jit(solution)/shard_map/gather_shards/pallas_call | solution.py:162
  130.9 0.7 dynamic-slice_add_fusion
  131.7 0.7 all_to_all.20
  132.3 6.4 %all-to-all-start = ((f32[8,1,1344]{2,1,0:T(1,128)}), f32[8,1,1344]{2,1,0:T(1,128)S(1)}, u32[]{:S(2)}, u32[]{:S(2)}) async-start(f32[8,1,1344]{2,1,0:T(1,128)} %all_to_all.20), calls=%async_computation | async-start | bytes 90112 | tf_op jit(solution)/shard_map/all_to_all | solution.py:534
  138.7 0.7 constant_dynamic-update-slice_fusion.15
  139.3 5.1 %all-to-all-done = f32[8,1,1344]{2,1,0:T(1,128)S(1)} async-done(((f32[8,1,1344]{2,1,0:T(1,128)}), f32[8,1,1344]{2,1,0:T(1,128)S(1)}, u32[]{:S(2)}, u32[]{:S(2)}) %all-to-all-start) | async-done | bytes 43040 | tf_op jit(solution)/shard_map/all_to_all | solution.py:534
  144.6 0.7 fusion.68
  145.2 0.7 slice.260
  146.0 0.6 slice_reduce_fusion.1
  147.6 3.8 %fusion.73 = f32[256,3072]{1,0:T(8,128)S(1)} fusion(bf16[256,768]{1,0:T(8,128)(2,1)S(1)} %fusion.26, bf16[768,3072]{1,0:T(8,128)(2,1)} %get-tuple-element.19), kind=kOutput, calls=%fused_computation.171 | convolution fusion | flops 1207959552 | bytes 8257536 | tf_op jit(solution)/shard_map/dot_general | solution.py:373
  151.4 1.6 fusion.65
  153.1 3.2 concatenate.57
  157.1 2.8 fusion.72
  160.0 2.4 convolution_convert_fusion.5
  162.4 0.7 slice-done.1
  163.1 1.4 fusion.74
  164.9 0.7 add.133
  165.9 0.9 fusion.62
  167.1 0.7 add.142
  167.8 4.0 %convolution_add_fusion = f32[256,3072]{1,0:T(8,128)S(1)} fusion(bf16[768,3072]{1,0:T(8,128)(2,1)} %get-tuple-element.20, f32[3072]{0:T(1024)S(1)} %add.142, f32[256,768]{1,0:T(8,128)S(1)} %get-tuple-element.45, f32[768]{0:T(1024)} %get-tuple-element.36, f32[768]{0:T(1024)} %get-tuple-element.37, f32[256]{0:T(256)S(1)} %add_rsqrt_fusion, ...), kind=kOutput, calls=%fused_computation.6 | convolution fusion | flops 1209729024 | bytes 8671232 | tf_op jit(solution)/shard_map/dot_general | solution.py:396
  171.9 8.2 %convert_reduce_fusion = (f32[3072]{0:T(1024)}, bf16[256,3072]{1,0:T(8,128)(2,1)S(1)}) fusion(f32[256,3072]{1,0:T(8,128)S(1)} %convolution_add_fusion, bf16[768,3072]{1,0:T(8,128)(2,1)} %get-tuple-element.21, bf16[1,256,768]{2,1,0:T(8,128)(2,1)S(1)} %copy-done.45, f32[]{:T(128)} %bitcast, f32[768]{0:T(1024)S(1)} %copy-done.43), kind=kOutput, calls=%fused_computation.17 | convolution fusion | flops 1226044416 | bytes 9845764 | tf_op jit(solution)/shard_map/dot_general | solution.py:408
  180.0 1.2 copy-done.6
  181.3 3.0 multiply_reduce_fusion.2
  184.4 7.4 %convert_reduce_fusion.3 = (f32[768]{0:T(1024)}, f32[768]{0:T(1024)}, bf16[1,256,768]{2,1,0:T(8,128)(2,1)}, f32[768]{0:T(1024)}, bf16[256,768]{1,0:T(8,128)(2,1)S(1)}, /*index=5*/f32[256,768]{1,0:T(8,128)}) fusion(bf16[1,256,768]{2,1,0:T(8,128)(2,1)S(1)} %copy-done.45, f32[]{:T(128)} %bitcast, f32[768]{0:T(1024)S(1)} %copy-done.43, ...), kind=kOutput, calls=%fused_computation.64 | convolution fusion | flops 1219950336 | bytes 11428868 | tf_op jit(solution)/shard_map/dot_general | solution.py:336
  192.6 0.7 constant_dynamic-update-slice_fusion.13
  194.0 0.7 constant_dynamic-update-slice_fusion.11
  195.4 0.7 constant_dynamic-update-slice_fusion.9
  196.8 0.7 constant_dynamic-update-slice_fusion.7
  198.2 0.7 constant_dynamic-update-slice_fusion.5
  199.6 0.7 constant_dynamic-update-slice_fusion.3
  201.0 0.7 constant_dynamic-update-slice_fusion.1
  202.4 5.0 %convolution_convert_fusion.4 = bf16[256,768]{1,0:T(8,128)(2,1)} fusion(bf16[256,3072]{0,1:T(8,128)(2,1)} %constant_dynamic-update-slice_fusion, bf16[768,3072]{1,0:T(8,128)(2,1)} %get-tuple-element.19), kind=kOutput, calls=%fused_computation.32 | convolution fusion | flops 1208156160 | bytes 6684672 | tf_op jit(solution)/shard_map/dot_general | solution.py:336
  207.4 1.2 copy.97
  208.6 2.7 multiply_reduce_fusion
  214.3 1.9 copy.103
  216.2 5.3 %convolution_convert_fusion.1.refs_1_ = bf16[768,3072]{1,0:T(8,128)(2,1)} fusion(bf16[256,3072]{1,0:T(8,128)(2,1)} %copy-done.6, f32[256,768]{1,0:T(8,128)S(1)} %get-tuple-element.45, f32[768]{0:T(1024)S(1)} %copy-done.15, f32[768]{0:T(1024)S(1)} %copy-done.17, f32[256]{0:T(256)S(1)} %copy-done.37, f32[256]{0:T(256)S(1)} %copy-done.29), kind=kOutput, calls=%fused_computation.2 | convolution fusion | flops 1211301888 | bytes 7086080 | tf_op jit(solution)/shard_map/dot_general | solution.py:326
  221.6 3.9 %convolution_convert_fusion.refs_2_ = bf16[768,3072]{1,0:T(8,128)(2,1)} fusion(bf16[1,256,768]{2,1,0:T(8,128)(2,1)S(1)} %copy-done.46, f32[]{:T(128)} %bitcast, f32[768]{0:T(1024)S(1)} %copy-done.44, f32[256,3072]{1,0:T(8,128)S(1)} %copy-done.48), kind=kOutput, calls=%fused_computation.1 | convolution fusion | flops 1218183168 | bytes 8260612 | tf_op jit(solution)/shard_map/dot_general | solution.py:326
  226.5 1.7 fusion.32
  228.3 1.1 multiply_reduce_fusion.3
  230.1 0.7 all_to_all.23
  230.7 3.3 all-to-all-start.1
  234.1 6.7 %convolution_convert_fusion.2.refs_0_ = bf16[768,3072]{1,0:T(8,128)(2,1)} fusion(bf16[256,3072]{0,1:T(8,128)(2,1)} %constant_dynamic-update-slice_fusion, bf16[256,3072]{0,1:T(8,128)(2,1)} %copy-done.30, bf16[256,768]{1,0:T(8,128)(2,1)S(1)} %copy-done.12, bf16[256,768]{1,0:T(8,128)(2,1)S(1)} %copy-done.9), kind=kOutput, calls=%fused_computation.3 | convolution fusion | flops 2426142720 | bytes 8650752 | tf_op jit(solution)/shard_map/dot_general | solution.py:326
  240.8 66.5 %scatter_shards.1 = (f32[192,384]{1,0:T(8,128)S(1)}, f32[192,384]{1,0:T(8,128)S(1)}, f32[96,768]{1,0:T(8,128)S(1)}) custom-call(bf16[768,3072]{1,0:T(8,128)(2,1)} %convolution_convert_fusion.2.refs_0_, bf16[768,3072]{1,0:T(8,128)(2,1)} %convolution_convert_fusion.1.refs_1_, bf16[768,3072]{1,0:T(8,128)(2,1)} %convolution_convert_fusion.refs_2_), custom_call_target="tpu_custom_call" | custom-call | tf_op jit(solution)/shard_map/scatter_shards/pallas_call | solution.py:296
  307.2 0.7 slice.233
  308.0 8.7 %all-gather = f32[32,1,1344]{2,1,0:T(1,128)S(1)} all-gather(f32[8,1,1344]{2,1,0:T(1,128)S(1)} %all-to-all-done.1), channel_id=2, replica_groups=mesh['dp'=4,'fsdp'=8] {'dp'}, dimensions={0}, use_global_device_ids=true | all-gather | bytes 215040 | tf_op jit(solution)/shard_map/all_gather | solution.py:564
  317.1 1.2 fusion.52
  318.4 25.9 %all-reduce.1 = f32[4,8,192]{2,0,1:T(4,128)S(1)} all-reduce(f32[4,8,192]{2,0,1:T(4,128)S(1)} %copy.101), channel_id=4, replica_groups=mesh['dp'=4,'fsdp'=8] {'fsdp'}, use_global_device_ids=true, to_apply=%region_22.23.clone | all-reduce | flops 6144 | bytes 49152
  344.4 0.6 constant_dynamic-slice_fusion
  345.6 3.2 all-to-all-start.2
  350.7 0.6 slice.282
  351.4 2.2 all-to-all-done.2
  354.2 0.7 copy.158
  354.9 0.7 copy.159
  355.7 0.7 copy.160
  (208 shorter events, 17.3 us)
Async XLA Ops:
  7.2 45.1 %copy-start = (bf16[192,576]{1,0:T(8,128)(2,1)S(1)}, bf16[192,576]{1,0:T(8,128)(2,1)}, u32[]{:S(2)}) copy-start(bf16[192,576]{1,0:T(8,128)(2,1)} %param.18) | copy-start | bytes 663556
  7.2 139.4 %copy-start.1 = (bf16[1,256,768]{2,1,0:T(8,128)(2,1)S(1)}, bf16[1,256,768]{2,1,0:T(8,128)(2,1)}, u32[]{:S(2)}) copy-start(bf16[1,256,768]{2,1,0:T(8,128)(2,1)} %param.14) | copy-start | bytes 1179652
  7.2 123.7 %all-reduce.4.cloned.1.call-start = ((), (), s32[]{:S(2)}) async-start(), calls=%async_computation.3 | async-start | bytes 163840
  55.6 91.2 %copy-start.23 = (f32[256]{0:T(256)}, f32[256]{0:T(256)S(1)}, u32[]{:S(2)}) copy-start(f32[256]{0:T(256)S(1)} %broadcast_multiply_fusion.5) | copy-start | bytes 3076
  56.9 94.5 %copy-start.34 = (f32[256]{0:T(256)}, f32[256]{0:T(256)S(1)}, u32[]{:S(2)}) copy-start(f32[256]{0:T(256)S(1)} %add_rsqrt_fusion.1) | copy-start | bytes 3076
  132.3 12.2 %all-to-all-start = ((f32[8,1,1344]{2,1,0:T(1,128)}), f32[8,1,1344]{2,1,0:T(1,128)S(1)}, u32[]{:S(2)}, u32[]{:S(2)}) async-start(f32[8,1,1344]{2,1,0:T(1,128)} %all_to_all.20), calls=%async_computation | async-start | bytes 90112 | tf_op jit(solution)/shard_map/all_to_all | solution.py:534
  146.6 0.6 copy-start.19
  146.9 0.7 copy-start.8
  156.8 3.2 copy-start.10
  157.1 5.3 %copy-start.4 = (bf16[256,768]{0,1:T(8,128)(2,1)}, bf16[256,768]{0,1:T(8,128)(2,1)S(1)}, u32[]{:S(2)}) copy-start(bf16[256,768]{0,1:T(8,128)(2,1)S(1)} %copy.87) | copy-start | bytes 1179652
  157.1 5.3 %slice-start = ((s8[4718592]{0:T(1024)(128)(4,1)}), s8[524288]{0:T(1024)(128)(4,1)S(1)}, s32[]{:S(2)}) async-start(s8[4718592]{0:T(1024)(128)(4,1)} %bitcast.126), calls=%async_computation.4 | async-start | bytes 1048576
  160.0 2.5 copy-start.21
  160.0 3.1 slice-start.1
  162.4 2.5 copy-start.3
  163.1 1.8 copy-start.27
  166.8 17.5 %copy-start.28 = (f32[256]{0:T(256)}, f32[256]{0:T(256)S(1)}, u32[]{:S(2)}) copy-start(f32[256]{0:T(256)S(1)} %broadcast_multiply_fusion.4) | copy-start | bytes 3076
  167.1 17.3 %copy-start.36 = (f32[256]{0:T(256)}, f32[256]{0:T(256)S(1)}, u32[]{:S(2)}) copy-start(f32[256]{0:T(256)S(1)} %add_rsqrt_fusion) | copy-start | bytes 3076
  167.8 4.0 %copy-start.43 = (f32[768]{0:T(1024)S(1)}, f32[768]{0:T(1024)}, u32[]{:S(2)}) copy-start(f32[768]{0:T(1024)} %get-tuple-element.35) | copy-start | bytes 9220
  167.8 4.0 %copy-start.45 = (bf16[1,256,768]{2,1,0:T(8,128)(2,1)S(1)}, bf16[1,256,768]{2,1,0:T(8,128)(2,1)}, u32[]{:S(2)}) copy-start(bf16[1,256,768]{2,1,0:T(8,128)(2,1)} %param.16) | copy-start | bytes 1179652
  167.8 13.4 %slice-start.4 = ((s8[4718592]{0:T(1024)(128)(4,1)}), s8[4194304]{0:T(1024)(128)(4,1)S(1)}, s32[]{:S(2)}) async-start(s8[4718592]{0:T(1024)(128)(4,1)} %bitcast.160), calls=%async_computation.8 | async-start | bytes 8388608
  171.8 8.2 %copy-start.47 = (f32[256,3072]{1,0:T(8,128)}, f32[256,3072]{1,0:T(8,128)S(1)}, u32[]{:S(2)}) copy-start(f32[256,3072]{1,0:T(8,128)S(1)} %convolution_add_fusion) | copy-start | bytes 9437188
  171.8 9.4 %copy-start.16 = (f32[768]{0:T(1024)S(1)}, f32[768]{0:T(1024)}, u32[]{:S(2)}) copy-start(f32[768]{0:T(1024)} %get-tuple-element.37) | copy-start | bytes 9220
  171.8 9.4 %slice-start.5 = ((s8[4718592]{0:T(1024)(128)(4,1)}), s8[524288]{0:T(1024)(128)(4,1)S(1)}, s32[]{:S(2)}) async-start(s8[4718592]{0:T(1024)(128)(4,1)} %bitcast.160), calls=%async_computation.9 | async-start | bytes 1048576
  180.0 1.2 copy-start.6
  181.2 3.0 copy-start.26
  181.2 3.1 copy-start.25
  202.4 6.2 %copy-start.11 = (bf16[256,768]{0,1:T(8,128)(2,1)S(1)}, bf16[256,768]{0,1:T(8,128)(2,1)}, u32[]{:S(2)}) copy-start(bf16[256,768]{0,1:T(8,128)(2,1)} %copy-done.10) | copy-start | bytes 1179652
  202.4 6.2 %copy-start.22 = (f32[12,256]{1,0:T(8,128)S(1)}, f32[12,256]{1,0:T(8,128)}, u32[]{:S(2)}) copy-start(f32[12,256]{1,0:T(8,128)} %copy-done.21) | copy-start | bytes 36868
  208.6 2.8 copy-start.13
  208.6 3.0 copy-start.2
  211.6 1.0 copy-start.5
  212.6 1.0 copy-start.14
  213.6 2.6 copy-start.15
  213.6 2.6 copy-start.17
  213.6 2.6 copy-start.29
  213.6 2.5 copy-start.37
  216.2 5.4 %copy-start.44 = (f32[768]{0:T(1024)S(1)}, f32[768]{0:T(1024)}, u32[]{:S(2)}) copy-start(f32[768]{0:T(1024)} %get-tuple-element.35) | copy-start | bytes 9220
  216.2 5.3 %copy-start.46 = (bf16[1,256,768]{2,1,0:T(8,128)(2,1)S(1)}, bf16[1,256,768]{2,1,0:T(8,128)(2,1)}, u32[]{:S(2)}) copy-start(bf16[1,256,768]{2,1,0:T(8,128)(2,1)} %param.16) | copy-start | bytes 1179652
  216.2 5.3 %copy-start.48 = (f32[256,3072]{1,0:T(8,128)S(1)}, f32[256,3072]{1,0:T(8,128)}, u32[]{:S(2)}) copy-start(f32[256,3072]{1,0:T(8,128)} %copy-done.47) | copy-start | bytes 9437188
  216.2 10.2 %slice-start.2 = ((s8[4718592]{0:T(1024)(128)(4,1)}), s8[4194304]{0:T(1024)(128)(4,1)S(1)}, s32[]{:S(2)}) async-start(s8[4718592]{0:T(1024)(128)(4,1)} %bitcast.128), calls=%async_computation.6 | async-start | bytes 8388608
  221.6 4.8 %slice-start.3 = ((s8[4718592]{0:T(1024)(128)(4,1)}), s8[524288]{0:T(1024)(128)(4,1)S(1)}, s32[]{:S(2)}) async-start(s8[4718592]{0:T(1024)(128)(4,1)} %bitcast.128), calls=%async_computation.7 | async-start | bytes 1048576
  225.5 0.9 copy-start.20
  225.5 0.9 copy-start.24
  225.5 0.9 copy-start.35
  226.4 1.7 copy-start.30
  226.4 1.8 copy-start.7
  226.5 1.8 copy-start.18
  228.2 1.3 copy-start.39
  228.2 1.3 copy-start.38
  228.2 1.3 copy-start.40
  228.2 1.6 copy-start.42
  228.2 1.7 copy-start.31
  228.2 1.7 copy-start.41
  228.2 5.8 %copy-start.9 = (bf16[256,768]{1,0:T(8,128)(2,1)S(1)}, bf16[256,768]{1,0:T(8,128)(2,1)}, u32[]{:S(2)}) copy-start(bf16[256,768]{1,0:T(8,128)(2,1)} %copy-done.8) | copy-start | bytes 1179652
  228.2 5.8 %copy-start.12 = (bf16[256,768]{1,0:T(8,128)(2,1)S(1)}, bf16[256,768]{1,0:T(8,128)(2,1)}, u32[]{:S(2)}) copy-start(bf16[256,768]{1,0:T(8,128)(2,1)} %copy.103) | copy-start | bytes 1179652
  230.7 77.3 %all-to-all-start.1 = ((f32[8,1,1344]{2,1,0:T(1,128)}), f32[8,1,1344]{2,1,0:T(1,128)S(1)}, u32[]{:S(2)}, u32[]{:S(2)}) async-start(f32[8,1,1344]{2,1,0:T(1,128)} %all_to_all.23), calls=%async_computation.1 | async-start | bytes 90112 | tf_op jit(solution)/shard_map/all_to_all | solution.py:563
  240.8 112.9 %copy-start.32 = (bf16[1,768]{1,0:T(2,128)(2,1)S(1)}, bf16[1,768]{1,0:T(2,128)(2,1)}, u32[]{:S(2)}) copy-start(bf16[1,768]{1,0:T(2,128)(2,1)} %param.15) | copy-start | bytes 4612
  240.8 112.9 %copy-start.33 = (f32[1,768]{1,0:T(1,128)S(1)}, f32[1,768]{1,0:T(1,128)}, u32[]{:S(2)}) copy-start(f32[1,768]{1,0:T(1,128)} %get-tuple-element.47) | copy-start | bytes 9220
  345.6 7.9 %all-to-all-start.2 = ((f32[4,1,192]{2,1,0:T(1,128)}), f32[4,1,192]{2,1,0:T(1,128)S(1)}, u32[]{:S(2)}, u32[]{:S(2)}) async-start(f32[4,1,192]{2,1,0:T(1,128)} %copy.102), calls=%async_computation.2 | async-start | bytes 8192 | tf_op jit(solution)/shard_map/all_to_all | solution.py:576
Sparse Core Ops, SparseCore 0:
  53.3 37.8 all-reduce.3
